TPU v7x, 32 devices: a whole 2x2x4 slice. The times are simulated.
32 devices in a mesh: section: 4 (over y, x), dp: 8 (over z, core).
Axes of the slice: x: 2, y: 2, z: 4, core: 2. Of those that a mesh axis runs over, the one named last changes fastest.
Arguments:
- tokens: bfloat16 [2048, 1024], P('dp', 'section'), may hold values from -6 to 6
- cotangent: bfloat16 [2048, 1024], P('dp', 'section'), may hold values from -6 to 6
- gains: float32 [4, 1024], P('section'), may hold values from 0.5 to 1.5
- attn_in: bfloat16 [4, 1024, 1536], P('section'), may hold values from -0.1875 to 0.1875
- attn_out: bfloat16 [4, 512, 1024], P('section'), may hold values from -0.75 to 0.75
- ffn_in: bfloat16 [4, 1024, 2816], P('section'), may hold values from -0.1875 to 0.1875
- ffn_out: bfloat16 [4, 1408, 1024], P('section'), may hold values from -0.15625 to 0.15625
- mix_level: int32 [16], replicated, may hold values from 1 to 7
- seq_lengths: int32 [16, 4], P('dp'), may hold values from 0 to 128, as said below
Outputs:
- outputs: bfloat16 [2048, 1024], P('dp', 'section')
- input_grad: float32 [2048, 1024], P('dp', 'section')
- gains_grad: float32 [4, 1024], P('section')
- attn_in_grad: float32 [4, 1024, 1536], P('section')
- attn_out_grad: float32 [4, 512, 1024], P('section')
- ffn_in_grad: float32 [4, 1024, 2816], P('section')
- ffn_out_grad: float32 [4, 1408, 1024], P('section')
- value_norm: float32 [], replicated
- blend_norm: float32 [], replicated
Inputs may be any that keep to these rules, and one draw needn't show every extreme that they name: `seq_lengths`: each row sums to 128; in every draw some row is a single sequence of 128 tokens; a length may be 0.
All inputs are finite; a program needn't handle non-finite values.
Results may differ from a plain program's by a relative error of at most 0.024.
Values may be sent and summed in bfloat16 or wider, within the bound.
No kernel may reach another device: no remote copies, remote signals or barrier semaphores. Data moves between devices by JAX's collectives and lax.ppermute only.
A program may use at most 256 MiB of HBM per device.

v0:
```python
import jax
import jax.numpy as jnp
from jax import lax
from jax.sharding import PartitionSpec as P

HEAD_DIM = 64


EPS = 1e-05
NEG = -1e30


def partner_2(value, axis, stride):
    mask = 2**stride
    pairs = [(source, source ^ mask) for source in range(lax.axis_size(axis))]
    return lax.ppermute(value, axis, pairs)


def as_sent(x):
    return jax.tree.map(lambda a: a.astype(jnp.bfloat16) if a.dtype == jnp.float32 else a, x)


def shifted(x, axis, by):
    peers = lax.axis_size(axis)
    pairs = [(i, i + by) for i in range(peers) if 0 <= i + by < peers]
    return lax.ppermute(x, axis, pairs)


def segment_of(lengths_row, count):
    ends = jnp.cumsum(lengths_row)
    places = jnp.arange(count, dtype=jnp.int32)
    return jnp.sum((places[:, None] >= ends[None, :]).astype(jnp.int32), axis=1)


def normalize(stream, norm_gain):
    rscale = lax.rsqrt(jnp.mean(stream * stream, axis=-1, keepdims=True) + EPS)
    normed = stream * rscale
    return ((normed * norm_gain).astype(jnp.bfloat16), normed, rscale)


def norm_back(dact, normed, rscale, norm_gain):
    dnorm = dact * norm_gain
    dgain = jnp.sum(dact * normed, axis=0)
    return (rscale * (dnorm - normed * jnp.mean(dnorm * normed, axis=-1, keepdims=True)), dgain)


def contract_rows(left, right):
    return lax.dot_general(
        left, right, (((0,), (0,)), ((), ())), preferred_element_type=jnp.float32
    )


def contract_cols(left, right):
    return lax.dot_general(
        left, right, (((1,), (1,)), ((), ())), preferred_element_type=jnp.float32
    )


def block_scores(query, keys, segments, start, block_rows):
    total = keys.shape[0]
    row_place = start + jnp.arange(block_rows, dtype=jnp.int32)
    col_place = jnp.arange(total, dtype=jnp.int32)
    row_segment = lax.dynamic_slice_in_dim(segments, start, block_rows)
    allowed = (col_place[None, :] <= row_place[:, None]) & (
        row_segment[:, None] == segments[None, :]
    )
    query_block = lax.dynamic_slice_in_dim(query, start, block_rows, 0)
    scores = jnp.einsum("qhd,khd->hqk", query_block, keys, preferred_element_type=jnp.float32)
    scores = scores * query.shape[2] ** (-0.5)
    return (jnp.where(allowed[None], scores, NEG), query_block)


def attend_forward(query, keys, values, segments):
    total = query.shape[0]
    block_rows = min(512, total)

    def one_block(index):
        scores, unused = block_scores(query, keys, segments, index * block_rows, block_rows)
        row_top = jnp.max(scores, axis=-1, keepdims=True)
        exponent = jnp.exp(scores - row_top)
        summed = jnp.sum(exponent, axis=-1, keepdims=True)
        attn_probs = (exponent / summed).astype(jnp.bfloat16)
        result = jnp.einsum("hqk,khd->qhd", attn_probs, values, preferred_element_type=jnp.float32)
        return (result, (row_top + jnp.log(summed))[:, :, 0])

    results, log_sums = lax.map(one_block, jnp.arange(total // block_rows))
    return (results.reshape(total, -1), log_sums)


def attend_back(query, keys, values, segments, dattn, log_sums):
    total = query.shape[0]
    block_rows = min(512, total)
    scale = query.shape[2] ** (-0.5)

    def one_block(carry, index):
        grad_keys, grad_values = carry
        start = index * block_rows
        scores, query_block = block_scores(query, keys, segments, start, block_rows)
        attn_probs = jnp.exp(scores - log_sums[index][:, :, None])
        dattn_block = lax.dynamic_slice_in_dim(dattn, start, block_rows, 0)
        dweights = jnp.einsum(
            "qhd,khd->hqk", dattn_block, values, preferred_element_type=jnp.float32
        )
        row_delta = jnp.sum(dweights * attn_probs, axis=-1, keepdims=True)
        dscores = (attn_probs * (dweights - row_delta)).astype(jnp.bfloat16)
        grad_query = (
            jnp.einsum("hqk,khd->qhd", dscores, keys, preferred_element_type=jnp.float32) * scale
        )
        grad_keys = (
            grad_keys
            + jnp.einsum("hqk,qhd->khd", dscores, query_block, preferred_element_type=jnp.float32)
            * scale
        )
        grad_values = grad_values + jnp.einsum(
            "hqk,qhd->khd",
            attn_probs.astype(jnp.bfloat16),
            dattn_block,
            preferred_element_type=jnp.float32,
        )
        return ((grad_keys, grad_values), grad_query)

    zeros_kv = jnp.zeros(keys.shape, jnp.float32)
    (grad_keys, grad_values), grad_query = lax.scan(
        one_block, (zeros_kv, zeros_kv), jnp.arange(total // block_rows)
    )
    return (
        grad_query.reshape(total, -1),
        grad_keys.reshape(total, -1),
        grad_values.reshape(total, -1),
    )


def attention_forward(
    section_input, first_low, attn_inward, attn_outward, norm_gain, mix_weight, mixing, segments
):
    stream = section_input.astype(jnp.float32)
    normed_act, normed, rscale = normalize(stream, norm_gain)
    projected = jnp.dot(normed_act, attn_inward, preferred_element_type=jnp.float32)
    width = attn_outward.shape[0]
    query = projected[:, :width].astype(jnp.bfloat16)
    keys = projected[:, width : 2 * width].astype(jnp.bfloat16)
    values = projected[:, 2 * width :].astype(jnp.bfloat16)
    values_wide = values.astype(jnp.float32)
    mixed = jnp.where(
        mixing,
        (1.0 - mix_weight) * values_wide + mix_weight * first_low.astype(jnp.float32),
        values_wide,
    ).astype(jnp.bfloat16)
    shape = (section_input.shape[0], -1, HEAD_DIM)
    results, log_sums = attend_forward(
        query.reshape(shape), keys.reshape(shape), mixed.reshape(shape), segments
    )
    attn = results.astype(jnp.bfloat16)
    section_output = stream + jnp.dot(attn, attn_outward, preferred_element_type=jnp.float32)
    return (section_output, values, (query, keys, mixed, attn, log_sums))


def attention_backward(
    section_input,
    kept,
    grad_out,
    dfirst_low,
    attn_inward,
    attn_outward,
    norm_gain,
    mix_weight,
    mixing,
    segments,
    totals,
):
    query, keys, mixed, attn, log_sums = kept
    grad_inward, grad_outward, grad_feed_in, grad_feed_out, grad_gain = totals
    normed_act, normed, rscale = normalize(section_input.astype(jnp.float32), norm_gain)
    count, width = attn.shape
    shape = (count, -1, HEAD_DIM)
    grad_outward = grad_outward + contract_rows(attn, grad_out)
    dattn = contract_cols(grad_out, attn_outward).astype(jnp.bfloat16)
    grad_query, grad_keys, grad_mixed = attend_back(
        query.reshape(shape),
        keys.reshape(shape),
        mixed.reshape(shape),
        segments,
        dattn.reshape(shape),
        log_sums,
    )
    grad_values = jnp.where(
        mixing, (1.0 - mix_weight) * grad_mixed, grad_mixed + dfirst_low.astype(jnp.float32)
    )
    send_first = (mix_weight * grad_mixed).astype(jnp.bfloat16)
    grad_proj = jnp.concatenate([grad_query, grad_keys, grad_values], axis=1).astype(jnp.bfloat16)
    grad_inward = grad_inward + contract_rows(normed_act, grad_proj)
    dact = contract_cols(grad_proj, attn_inward)
    grad_stream, dgain = norm_back(dact, normed, rscale, norm_gain)
    new_totals = (grad_inward, grad_outward, grad_feed_in, grad_feed_out, grad_gain + dgain)
    return (grad_out.astype(jnp.float32) + grad_stream, send_first, new_totals)


def feed_forward(section_input, feed_inward, feed_outward, norm_gain):
    stream = section_input.astype(jnp.float32)
    normed_act, normed, rscale = normalize(stream, norm_gain)
    both = jnp.dot(normed_act, feed_inward, preferred_element_type=jnp.float32)
    hidden_units = feed_outward.shape[0]
    gate_pre = both[:, :hidden_units]
    up_pre = both[:, hidden_units:]
    hidden = (jax.nn.silu(gate_pre) * up_pre).astype(jnp.bfloat16)
    return (
        stream + jnp.dot(hidden, feed_outward, preferred_element_type=jnp.float32),
        (gate_pre, up_pre),
    )


def feed_backward(section_input, kept, grad_out, feed_inward, feed_outward, norm_gain, totals):
    gate_pre, up_pre = kept
    grad_inward, grad_outward, grad_feed_in, grad_feed_out, grad_gain = totals
    normed_act, normed, rscale = normalize(section_input.astype(jnp.float32), norm_gain)
    sigmoid_gate = jax.nn.sigmoid(gate_pre)
    swish_gate = jax.nn.silu(gate_pre)
    hidden = (swish_gate * up_pre).astype(jnp.bfloat16)
    grad_feed_out = grad_feed_out + contract_rows(hidden, grad_out)
    grad_hidden = contract_cols(grad_out, feed_outward)
    grad_gate = grad_hidden * up_pre * sigmoid_gate * (1.0 + gate_pre * (1.0 - sigmoid_gate))
    grad_up = grad_hidden * swish_gate
    grad_both = jnp.concatenate([grad_gate, grad_up], axis=1).astype(jnp.bfloat16)
    grad_feed_in = grad_feed_in + contract_rows(normed_act, grad_both)
    dact = contract_cols(grad_both, feed_inward)
    grad_stream, dgain = norm_back(dact, normed, rscale, norm_gain)
    new_totals = (grad_inward, grad_outward, grad_feed_in, grad_feed_out, grad_gain + dgain)
    return (grad_out.astype(jnp.float32) + grad_stream, new_totals)


def body(tokens, cotangent, gains, attn_in, attn_out, ffn_in, ffn_out, mix_level, seq_lengths):
    sections = lax.axis_size("section")
    section_index = lax.axis_index("section")
    section_kind = section_index % 2
    first_half = section_kind == 0
    mixing = section_index == 2
    own_pieces = (attn_in[0], attn_out[0], ffn_in[0], ffn_out[0])
    partner = partner_2((attn_in[0], attn_out[0], ffn_in[0], ffn_out[0]), "section", 0)
    lower = [jnp.where(first_half, own, got) for own, got in zip(own_pieces, partner)]
    upper = [jnp.where(first_half, got, own) for own, got in zip(own_pieces, partner)]
    half_qk = attn_out.shape[1]
    width = 2 * half_qk
    attn_inward = jnp.concatenate(
        [
            lower[0][:, :half_qk],
            upper[0][:, :half_qk],
            lower[0][:, half_qk : 2 * half_qk],
            upper[0][:, half_qk : 2 * half_qk],
            lower[0][:, 2 * half_qk :],
            upper[0][:, 2 * half_qk :],
        ],
        axis=1,
    )
    attn_outward = jnp.concatenate([lower[1], upper[1]], axis=0)
    half_ff = ffn_out.shape[1]
    hidden_units = 2 * half_ff
    feed_inward = jnp.concatenate(
        [
            lower[2][:, :half_ff],
            upper[2][:, :half_ff],
            lower[2][:, half_ff:],
            upper[2][:, half_ff:],
        ],
        axis=1,
    )
    feed_outward = jnp.concatenate([lower[3], upper[3]], axis=0)
    norm_gain = gains[0]
    heads = width // HEAD_DIM
    mix_weight = jnp.repeat(mix_level.astype(jnp.float32) / 8.0, HEAD_DIM)
    inputs, grads_in = (
        lax.all_gather(tokens, "section", axis=1, tiled=True),
        lax.all_gather(cotangent, "section", axis=1, tiled=True),
    )
    micro = seq_lengths.shape[0]
    count = inputs.shape[0] // micro
    model = inputs.shape[1]
    segs = jnp.stack([segment_of(seq_lengths[index], count) for index in range(micro)])
    block_rows = min(512, count)
    blocks = count // block_rows

    def empty_attn():
        zero_cols = jnp.zeros((count, width), jnp.bfloat16)
        return (
            zero_cols,
            zero_cols,
            zero_cols,
            zero_cols,
            jnp.zeros((blocks, heads, block_rows), jnp.float32),
        )

    def empty_feed():
        zero_hidden = jnp.zeros((count, hidden_units), jnp.float32)
        return (zero_hidden, zero_hidden)

    def stacked(parts):
        return tuple((jnp.zeros((micro + 1,) + part.shape, part.dtype) for part in parts))

    kept_attn = stacked(empty_attn())
    kept_feed = stacked(empty_feed())
    kept_input = jnp.zeros((micro + 1, count, model), jnp.bfloat16)
    results = jnp.zeros((micro + 1, count, model), jnp.float32)

    def resting_forward(section_input, first_low, segments):
        return (
            jnp.zeros((count, model), jnp.float32),
            jnp.zeros((count, width), jnp.bfloat16),
            empty_attn(),
            empty_feed(),
        )

    def attn_forward(section_input, first_low, segments):
        section_output, values, kept = attention_forward(
            section_input,
            first_low,
            attn_inward,
            attn_outward,
            norm_gain,
            mix_weight,
            mixing,
            segments,
        )
        return (section_output, values, kept, empty_feed())

    def feed_forward_branch(section_input, first_low, segments):
        section_output, kept = feed_forward(section_input, feed_inward, feed_outward, norm_gain)
        return (section_output, first_low, empty_attn(), kept)

    moments = micro + sections - 1
    incoming = jnp.zeros((count, model), jnp.bfloat16)
    incoming_first = jnp.zeros((count, width), jnp.bfloat16)
    for moment in range(moments):
        micro_index = moment - section_index
        active = (micro_index >= 0) & (micro_index < micro)
        slot_pick = jnp.clip(micro_index, 0, micro - 1)
        slot_place = jnp.where(active, micro_index, micro)
        own_input = lax.dynamic_slice_in_dim(inputs, slot_pick * count, count, 0)
        section_input = jnp.where(section_index == 0, own_input, incoming)
        first_low = incoming_first
        branch = jnp.where(active, section_kind + 1, 0)
        section_output, first_out, new_attn, new_feed = lax.switch(
            branch,
            (resting_forward, attn_forward, feed_forward_branch),
            section_input,
            first_low,
            segs[slot_pick],
        )
        kept_input = kept_input.at[slot_place].set(section_input)
        kept_attn = tuple((buf.at[slot_place].set(part) for buf, part in zip(kept_attn, new_attn)))
        kept_feed = tuple((buf.at[slot_place].set(part) for buf, part in zip(kept_feed, new_feed)))
        results = results.at[slot_place].set(section_output)
        if moment < moments - 1:
            incoming, incoming_first = (
                shifted(section_output.astype(jnp.bfloat16), "section", 1),
                shifted(as_sent(first_out), "section", 1).astype(first_out.dtype),
            )
    mixed_kept = kept_attn[2][:micro].astype(jnp.float32)
    square_total = jnp.sum(mixed_kept * mixed_kept)
    value_part = jnp.where(section_index == 0, square_total, 0.0)
    blend_part = jnp.where(section_index == 2, square_total, 0.0)
    value_total, blend_total = lax.psum((value_part, blend_part), ("section", "dp"))
    entries = micro * count * lax.axis_size("dp") * width
    value_norm = value_total / entries
    blend_norm = blend_total / entries

    def resting_backward(section_input, kept_a, kept_f, grad_out, dfirst_low, segments, totals):
        return (
            jnp.zeros((count, model), jnp.float32),
            jnp.zeros((count, width), jnp.bfloat16),
            totals,
        )

    def attn_backward(section_input, kept_a, kept_f, grad_out, dfirst_low, segments, totals):
        return attention_backward(
            section_input,
            kept_a,
            grad_out,
            dfirst_low,
            attn_inward,
            attn_outward,
            norm_gain,
            mix_weight,
            mixing,
            segments,
            totals,
        )

    def feed_backward_branch(section_input, kept_a, kept_f, grad_out, dfirst_low, segments, totals):
        grad_input, new_totals = feed_backward(
            section_input, kept_f, grad_out, feed_inward, feed_outward, norm_gain, totals
        )
        return (grad_input, dfirst_low, new_totals)

    totals = (
        jnp.zeros(attn_inward.shape, jnp.float32),
        jnp.zeros(attn_outward.shape, jnp.float32),
        jnp.zeros(feed_inward.shape, jnp.float32),
        jnp.zeros(feed_outward.shape, jnp.float32),
        jnp.zeros((model,), jnp.float32),
    )
    dinputs = jnp.zeros((micro + 1, count, model), jnp.float32)
    incoming = jnp.zeros((count, model), jnp.bfloat16)
    incoming_first = jnp.zeros((count, width), jnp.bfloat16)
    for moment in range(moments):
        micro_index = moment - (sections - 1 - section_index)
        active = (micro_index >= 0) & (micro_index < micro)
        slot_pick = jnp.clip(micro_index, 0, micro - 1)
        slot_place = jnp.where(active, micro_index, micro)
        own_grad = lax.dynamic_slice_in_dim(grads_in, slot_pick * count, count, 0)
        grad_out = jnp.where(section_index == sections - 1, own_grad, incoming)
        dfirst_low = incoming_first
        branch = jnp.where(active, section_kind + 1, 0)
        grad_input, dfirst_out, totals = lax.switch(
            branch,
            (resting_backward, attn_backward, feed_backward_branch),
            kept_input[slot_place],
            tuple((buf[slot_place] for buf in kept_attn)),
            tuple((buf[slot_place] for buf in kept_feed)),
            grad_out,
            dfirst_low,
            segs[slot_pick],
            totals,
        )
        dinputs = dinputs.at[slot_place].set(grad_input)
        if moment < moments - 1:
            incoming, incoming_first = (
                shifted(grad_input.astype(jnp.bfloat16), "section", -1),
                shifted(as_sent(dfirst_out), "section", -1).astype(dfirst_out.dtype),
            )
    final_rows = jnp.where(
        section_index == sections - 1, results[:micro].reshape(micro * count, model), 0.0
    )
    input_rows = jnp.where(section_index == 0, dinputs[:micro].reshape(micro * count, model), 0.0)
    out_part, dinput_part = (
        lax.psum_scatter(
            final_rows.astype(jnp.bfloat16), "section", scatter_dimension=1, tiled=True
        ).astype(jnp.float32),
        lax.psum_scatter(
            input_rows.astype(jnp.bfloat16), "section", scatter_dimension=1, tiled=True
        ).astype(jnp.float32),
    )
    grad_inward, grad_outward, grad_feed_in, grad_feed_out, grad_gain = totals

    def inward_half(part):
        return jnp.concatenate(
            [
                grad_inward[
                    :, block * width + part * half_qk : block * width + (part + 1) * half_qk
                ]
                for block in range(3)
            ],
            axis=1,
        )

    def feed_half(part):
        return jnp.concatenate(
            [
                grad_feed_in[:, part * half_ff : (part + 1) * half_ff],
                grad_feed_in[
                    :, hidden_units + part * half_ff : hidden_units + (part + 1) * half_ff
                ],
            ],
            axis=1,
        )

    full_in = jnp.stack([inward_half(0), inward_half(1)])
    full_out = grad_outward.reshape(2, half_qk, model)
    full_feed_in = jnp.stack([feed_half(0), feed_half(1)])
    full_feed_out = grad_feed_out.reshape(2, half_ff, model)
    other_kind = 1 - section_kind
    fulls = (full_in, full_out, full_feed_in, full_feed_out)
    owned = [lax.dynamic_index_in_dim(part, section_kind, 0, keepdims=True) for part in fulls]
    sent = [lax.dynamic_index_in_dim(part, other_kind, 0, keepdims=True) for part in fulls]
    got = partner_2(
        (as_sent(sent[0]), as_sent(sent[1]), as_sent(sent[2]), as_sent(sent[3])), "section", 0
    )
    d_gain, d_in, d_out, d_feed_in, d_feed_out = (
        lax.psum(grad_gain[None].astype(jnp.bfloat16), "dp").astype(jnp.float32),
        lax.psum((owned[0] + got[0]).astype(jnp.bfloat16), "dp").astype(jnp.float32),
        lax.psum((owned[1] + got[1]).astype(jnp.bfloat16), "dp").astype(jnp.float32),
        lax.psum((owned[2] + got[2]).astype(jnp.bfloat16), "dp").astype(jnp.float32),
        lax.psum((owned[3] + got[3]).astype(jnp.bfloat16), "dp").astype(jnp.float32),
    )
    return (
        out_part.astype(jnp.bfloat16),
        dinput_part,
        d_gain,
        d_in,
        d_out,
        d_feed_in,
        d_feed_out,
        value_norm,
        blend_norm,
    )


def solution(mesh):
    in_specs = (
        P("dp", "section"),
        P("dp", "section"),
        P("section", None),
        P("section", None, None),
        P("section", None, None),
        P("section", None, None),
        P("section", None, None),
        P(),
        P("dp", None),
    )
    out_specs = (
        P("dp", "section"),
        P("dp", "section"),
        P("section", None),
        P("section", None, None),
        P("section", None, None),
        P("section", None, None),
        P("section", None, None),
        P(),
        P(),
    )
    return jax.shard_map(body, mesh=mesh, in_specs=in_specs, out_specs=out_specs, check_vma=False)
```

profile of v0, /device:TPU:0, one launch (start us, length us, event | category | flops | bytes accessed | tf_op | source)
XLA Modules:
  0.0 1427.5 jit_solution(1600875850976585298)
XLA Ops:
  14.6 279.9 %all_gather.6 = bf16[256,1024]{1,0:T(8,128)(2,1)S(1)} all-gather(bf16[256,256]{1,0:T(8,128)(2,1)} %param.139), channel_id=1, replica_groups=mesh['section'=4,'dp'=8] {'section'}, dimensions={1}, use_global_device_ids=true | all-gather | bytes 655360 | tf_op jit(solution)/shard_map/all_gather | solution.py:271
  294.5 12.1 all_gather.7
  333.4 9.5 broadcast_select_fusion.1
  347.7 8.3 pad_maximum_fusion.30
  356.0 23.2 %conditional.10 = (bf16[128,1024]{1,0:T(8,128)(2,1)}, bf16[128,1024]{1,0:T(8,128)(2,1)}, bf16[128,1024]{1,0:T(8,128)(2,1)}, bf16[128,1024]{1,0:T(8,128)(2,1)}, b...) conditional(s32[]{:T(128)} %clamp.30, () %tuple.501, ...), branch_computations={%region_5.6_spmd, %region_6.10_spmd, %region_10.12_spmd} | conditional | flops 2218065920 | bytes 48511104 | solution.py:340
  396.9 21.4 %conditional.11 = (bf16[128,1024]{1,0:T(8,128)(2,1)}, bf16[128,1024]{1,0:T(8,128)(2,1)}, bf16[1,128,1024]{2,1,0:T(8,128)(2,1)}, bf16[1,128,1024]{2,1,0:T(8,128)(...) conditional(s32[]{:T(128)} %clamp.31, () %tuple.504, ...), branch_computations={%region_13.14_spmd, %region_14.18_spmd, %region_18.20_spmd} | conditional | flops 2218065920 | bytes 50870456 | solution.py:340
  438.3 13.7 conditional.12
  471.9 6.9 conditional.13
  480.1 8.9 collective-permute-start.11
  505.7 10.2 conditional.14
  533.4 32.7 %conditional.15 = (bf16[128,1024]{1,0:T(8,128)(2,1)}, bf16[128,1024]{0,1:T(8,128)(2,1)}, f32[1024,3072]{1,0:T(8,128)}, f32[1024,1024]{1,0:T(8,128)}, f32[1024,56...) conditional(s32[]{:T(128)} %clamp.35, () %tuple.516, ...), branch_computations={%region_51.52_spmd, %region_52.57_spmd, %region_57.61_spmd} | conditional | flops 4444814336 | bytes 131487400 | solution.py:412
  534.9 6.1 broadcast_in_dim.432
  543.6 10.6 broadcast_in_dim.434
  568.8 6.1 collective-permute-done.12
  577.6 7.9 conditional.16
  597.6 7.7 conditional.17
  607.9 82.7 %collective-permute-done.16 = bf16[128,1024]{1,0:T(8,128)(2,1)} collective-permute-done((bf16[128,1024]{1,0:T(8,128)(2,1)}, bf16[128,1024]{1,0:T(8,128)(2,1)}, u32[]{:S(2)}, u32[]{:S(2)}) %collective-permute-start.16) | collective-permute-done | bytes 262176 | tf_op jit(solution)/shard_map/ppermute | solution.py:26
  694.0 51.4 %conditional.18 = (bf16[128,1024]{1,0:T(8,128)(2,1)}, bf16[128,1024]{0,1:T(8,128)(2,1)}, f32[1024,3072]{1,0:T(8,128)}, f32[1024,1024]{1,0:T(8,128)}, f32[1024,56...) conditional(s32[]{:T(128)} %clamp.38, (f32[1024,3072]{1,0:T(8,128)}, ...), branch_computations={%region_84.85_spmd, %region_85.90_spmd, %region_90.94_spmd} | conditional | flops 4453466112 | bytes 149587648 | solution.py:412
  722.8 11.1 convolution_add_fusion.18
  756.9 40.1 %conditional.19 = (f32[1024,3072]{1,0:T(8,128)}, f32[1024,1024]{1,0:T(8,128)}, f32[1024,5632]{1,0:T(8,128)}, f32[2816,1024]{1,0:T(8,128)}, f32[1024]{0:T(1024)S(1)}, /*index=5*/bf16[1,128,1024]{2,1,0:T(8,128)(2,1)S(1)}) conditional(s32[]{:T(128)} %clamp.39, (f32[1024,3072]{1,0:T(8,128)}, f32[1024,1024]{1,0:T(8,128)}, ...), branch_computations={%region_95.96_spmd, %region_96.101_spmd, %region_101.105_spmd} | conditional | flops 4453466112 | bytes 145917520 | solution.py:412
  769.4 11.1 convolution_add_fusion.22
  797.0 16.3 %fusion.439 = (f32[1024,1408]{1,0:T(8,128)}, f32[1024,1408]{1,0:T(8,128)}, f32[1024,1408]{1,0:T(8,128)}, f32[1024,1408]{1,0:T(8,128)}) fusion(f32[1024,5632]{1,0:T(8,128)} %get-tuple-element.3046), kind=kLoop, calls=%fused_computation.868 | loop fusion | bytes 46137344 | tf_op jit(solution)/shard_map/slice | solution.py:457
  813.3 9.6 maximum_bitcast_fusion
  822.9 9.4 maximum_bitcast_fusion.1
  832.3 7.9 fusion.407
  846.9 8.8 fusion.440
  880.5 233.9 %collective-permute-done.21 = bf16[1,512,1024]{2,1,0:T(8,128)(2,1)S(1)} collective-permute-done((bf16[1,512,1024]{2,1,0:T(8,128)(2,1)}, bf16[1,512,1024]{2,1,0:T(8,128)(2,1)S(1)}, u32[]{:S(2)}, u32[]{:S(2)}) %collective-permute-start.21) | collective-permute-done | bytes 1048608 | tf_op jit(solution)/shard_map/ppermute | solution.py:16
  1117.4 6.3 add_convert_fusion
  1129.2 9.6 fusion.410
  1150.4 41.2 %all-reduce = (f32[]{:T(128)}, f32[]{:T(128)}) all-reduce(f32[]{:T(128)S(6)} %select_n.660, f32[]{:T(128)S(6)} %select_n.661), channel_id=1, replica_groups=mesh['section'=4,'dp'=8] {'section','dp'}, use_global_device_ids=true, to_apply=%region_112.113 | all-reduce | flops 2 | bytes 16 | tf_op jit(solution)/shard_map/psum | solution.py:360
  1192.9 16.4 %psum.49 = bf16[1,1024]{1,0:T(2,128)(2,1)S(1)} all-reduce(bf16[1,1024]{1,0:T(2,128)(2,1)S(1)} %convert_element_type.790), channel_id=1, replica_groups=mesh['section'=4,'dp'=8] {'dp'}, use_global_device_ids=true, to_apply=%region_106.107 | all-reduce | flops 1024 | bytes 4096 | tf_op jit(solution)/shard_map/psum | solution.py:477
  1211.5 190.0 %all-reduce.4.cloned.1.call-done = (bf16[1,1024,1536]{2,1,0:T(8,128)(2,1)}, bf16[1,512,1024]{2,1,0:T(8,128)(2,1)}, bf16[1,1024,2816]{2,1,0:T(8,128)(2,1)}, bf16[1,1408,1024]{2,1,0:T(8,128)(2,1)}) async-done(((bf16[1,1024,1536]{2,1,0:T(8,128)(2,1)}, bf16[1,512,1024]{2,1,0:T(8,128)(2,1)}, bf16[1,1024,2816]{2,1,0:T(8,128)(2,1)}, bf16[1,1408,1024]{2,1,0:T(8,128)(2,1)}), (bf16[1,1024,1536]{2,1,0:T(8,128)(2,1)}, ...) | async-done | bytes 12845072 | tf_op jit(solution)/shard_map/psum | solution.py:478
  (435 shorter events, 359.5 us)
Async XLA Ops:
  8.0 308.1 %copy-start.89 = (bf16[1,512,1024]{2,1,0:T(8,128)(2,1)S(1)}, bf16[1,512,1024]{2,1,0:T(8,128)(2,1)}, u32[]{:S(2)}) copy-start(bf16[1,512,1024]{2,1,0:T(8,128)(2,1)} %param.143) | copy-start | bytes 3145732
  8.0 1201.9 %reduce-scatter.5.cloned.1.call-start = ((), (), s32[]{:S(2)}) async-start(), calls=%async_computation.3 | async-start | bytes 655360 | tf_op jit(solution)/shard_map/reduce_scatter | solution.py:437
  8.1 309.9 %collective-permute-start.3 = (bf16[1408,1024]{1,0:T(8,128)(2,1)}, bf16[1408,1024]{1,0:T(8,128)(2,1)}, u32[]{:S(2)}, u32[]{:S(2)}) collective-permute-start(bf16[1408,1024]{1,0:T(8,128)(2,1)} %bitcast.733), channel_id=1, source_target_pairs={{0,8},{8,0},{16,24},{24,16},{1,9},{9,1},{17,25},{25,17},{2,10},{10... | collective-permute-start | bytes 8650760 | tf_op jit(solution)/shard_map/ppermute | solution.py:16
  11.1 313.8 %collective-permute-start = (bf16[1024,1536]{1,0:T(8,128)(2,1)}, bf16[1024,1536]{1,0:T(8,128)(2,1)}, u32[]{:S(2)}, u32[]{:S(2)}) collective-permute-start(bf16[1024,1536]{1,0:T(8,128)(2,1)} %bitcast.732), channel_id=1, source_target_pairs={{0,8},{8,0},{16,24},{24,16},{1,9},{9,1},{17,25},{25,17},{2,10},{10... | collective-permute-start | bytes 9437192 | tf_op jit(solution)/shard_map/ppermute | solution.py:16
  11.2 304.9 %collective-permute-start.1 = (bf16[512,1024]{1,0:T(8,128)(2,1)}, bf16[512,1024]{1,0:T(8,128)(2,1)}, u32[]{:S(2)}, u32[]{:S(2)}) collective-permute-start(bf16[512,1024]{1,0:T(8,128)(2,1)} %bitcast.766), channel_id=1, source_target_pairs={{0,8},{8,0},{16,24},{24,16},{1,9},{9,1},{17,25},{25,17},{2,10},{10... | collective-permute-start | bytes 3145736 | tf_op jit(solution)/shard_map/ppermute | solution.py:16
  13.1 320.3 %collective-permute-start.2 = (bf16[1024,2816]{1,0:T(8,128)(2,1)}, bf16[1024,2816]{1,0:T(8,128)(2,1)}, u32[]{:S(2)}, u32[]{:S(2)}) collective-permute-start(bf16[1024,2816]{1,0:T(8,128)(2,1)} %bitcast.731), channel_id=1, source_target_pairs={{0,8},{8,0},{16,24},{24,16},{1,9},{9,1},{17,25},{25,17},{2,10},{10... | collective-permute-start | bytes 17301512 | tf_op jit(solution)/shard_map/ppermute | solution.py:16
  294.5 23.2 %copy-start.64 = (bf16[256,1024]{1,0:T(8,128)(2,1)}, bf16[256,1024]{1,0:T(8,128)(2,1)S(1)}, u32[]{:S(2)}) copy-start(bf16[256,1024]{1,0:T(8,128)(2,1)S(1)} %all_gather.6) | copy-start | bytes 1572868
  379.2 15.9 %collective-permute-start.4 = (bf16[128,1024]{1,0:T(8,128)(2,1)}, bf16[128,1024]{1,0:T(8,128)(2,1)S(1)}, u32[]{:S(2)}, u32[]{:S(2)}) collective-permute-start(bf16[128,1024]{1,0:T(8,128)(2,1)} %get-tuple-element.2970), channel_id=1, source_target_pairs={{0,8},{8,16},{16,24},{1,9},{9,17},{17,25},{2,10},{10,18},{18,26},{... | collective-permute-start | bytes 786440 | tf_op jit(solution)/shard_map/ppermute | solution.py:26
  380.7 15.3 %collective-permute-start.5 = (bf16[128,1024]{1,0:T(8,128)(2,1)}, bf16[128,1024]{1,0:T(8,128)(2,1)S(1)}, u32[]{:S(2)}, u32[]{:S(2)}) collective-permute-start(bf16[128,1024]{1,0:T(8,128)(2,1)} %get-tuple-element.2971), channel_id=1, source_target_pairs={{0,8},{8,16},{16,24},{1,9},{9,17},{17,25},{2,10},{10,18},{18,26},{... | collective-permute-start | bytes 786440 | tf_op jit(solution)/shard_map/ppermute | solution.py:26
  418.3 18.3 %collective-permute-start.6 = (bf16[128,1024]{1,0:T(8,128)(2,1)}, bf16[128,1024]{1,0:T(8,128)(2,1)S(1)}, u32[]{:S(2)}, u32[]{:S(2)}) collective-permute-start(bf16[128,1024]{1,0:T(8,128)(2,1)} %get-tuple-element.2972), channel_id=1, source_target_pairs={{0,8},{8,16},{16,24},{1,9},{9,17},{17,25},{2,10},{10,18},{18,26},{... | collective-permute-start | bytes 786440 | tf_op jit(solution)/shard_map/ppermute | solution.py:26
  419.6 17.8 %collective-permute-start.7 = (bf16[128,1024]{1,0:T(8,128)(2,1)}, bf16[128,1024]{1,0:T(8,128)(2,1)S(1)}, u32[]{:S(2)}, u32[]{:S(2)}) collective-permute-start(bf16[128,1024]{1,0:T(8,128)(2,1)} %get-tuple-element.2973), channel_id=1, source_target_pairs={{0,8},{8,16},{16,24},{1,9},{9,17},{17,25},{2,10},{10,18},{18,26},{... | collective-permute-start | bytes 786440 | tf_op jit(solution)/shard_map/ppermute | solution.py:26
  452.1 18.2 %collective-permute-start.8 = (bf16[128,1024]{1,0:T(8,128)(2,1)}, bf16[128,1024]{1,0:T(8,128)(2,1)S(1)}, u32[]{:S(2)}, u32[]{:S(2)}) collective-permute-start(bf16[128,1024]{1,0:T(8,128)(2,1)} %get-tuple-element.2974), channel_id=1, source_target_pairs={{0,8},{8,16},{16,24},{1,9},{9,17},{17,25},{2,10},{10,18},{18,26},{... | collective-permute-start | bytes 786440 | tf_op jit(solution)/shard_map/ppermute | solution.py:26
  453.4 17.7 %collective-permute-start.9 = (bf16[128,1024]{1,0:T(8,128)(2,1)}, bf16[128,1024]{1,0:T(8,128)(2,1)S(1)}, u32[]{:S(2)}, u32[]{:S(2)}) collective-permute-start(bf16[128,1024]{1,0:T(8,128)(2,1)} %get-tuple-element.2975), channel_id=1, source_target_pairs={{0,8},{8,16},{16,24},{1,9},{9,17},{17,25},{2,10},{10,18},{18,26},{... | collective-permute-start | bytes 786440 | tf_op jit(solution)/shard_map/ppermute | solution.py:26
  478.8 25.3 %collective-permute-start.10 = (bf16[128,1024]{1,0:T(8,128)(2,1)}, bf16[128,1024]{1,0:T(8,128)(2,1)S(1)}, u32[]{:S(2)}, u32[]{:S(2)}) collective-permute-start(bf16[128,1024]{1,0:T(8,128)(2,1)} %get-tuple-element.2976), channel_id=1, source_target_pairs={{0,8},{8,16},{16,24},{1,9},{9,17},{17,25},{2,10},{10,18},{18,26},{... | collective-permute-start | bytes 786440 | tf_op jit(solution)/shard_map/ppermute | solution.py:26
  480.1 24.8 %collective-permute-start.11 = (bf16[128,1024]{1,0:T(8,128)(2,1)}, bf16[128,1024]{1,0:T(8,128)(2,1)S(1)}, u32[]{:S(2)}, u32[]{:S(2)}) collective-permute-start(bf16[128,1024]{1,0:T(8,128)(2,1)} %get-tuple-element.2977), channel_id=1, source_target_pairs={{0,8},{8,16},{16,24},{1,9},{9,17},{17,25},{2,10},{10,18},{18,26},{... | collective-permute-start | bytes 786440 | tf_op jit(solution)/shard_map/ppermute | solution.py:26
  566.1 8.7 collective-permute-start.12
  567.4 10.2 collective-permute-start.13
  585.6 8.6 collective-permute-start.14
  586.9 10.0 collective-permute-start.15
  597.6 96.4 %copy-start.20 = (bf16[128,1024]{1,0:T(8,128)(2,1)S(1)}, bf16[128,1024]{1,0:T(8,128)(2,1)}, u32[]{:S(2)}) copy-start(bf16[128,1024]{1,0:T(8,128)(2,1)} %get-tuple-element.3793) | copy-start | bytes 786436
  605.3 85.3 %collective-permute-start.16 = (bf16[128,1024]{1,0:T(8,128)(2,1)}, bf16[128,1024]{1,0:T(8,128)(2,1)}, u32[]{:S(2)}, u32[]{:S(2)}) collective-permute-start(bf16[128,1024]{1,0:T(8,128)(2,1)} %get-tuple-element.3028), channel_id=1, source_target_pairs={{8,0},{16,8},{24,16},{9,1},{17,9},{25,17},{10,2},{18,10},{26,18},{... | collective-permute-start | bytes 786440 | tf_op jit(solution)/shard_map/ppermute | solution.py:26
  606.6 86.7 %collective-permute-start.17 = (bf16[128,1024]{0,1:T(8,128)(2,1)}, bf16[128,1024]{0,1:T(8,128)(2,1)S(1)}, u32[]{:S(2)}, u32[]{:S(2)}) collective-permute-start(bf16[128,1024]{0,1:T(8,128)(2,1)} %get-tuple-element.3034), channel_id=1, source_target_pairs={{8,0},{16,8},{24,16},{9,1},{17,9},{25,17},{10,2},{18,10},{26,18},{... | collective-permute-start | bytes 786440 | tf_op jit(solution)/shard_map/ppermute | solution.py:26
  694.0 62.9 %copy-start.19 = (bf16[128,1024]{1,0:T(8,128)(2,1)S(1)}, bf16[128,1024]{1,0:T(8,128)(2,1)}, u32[]{:S(2)}) copy-start(bf16[128,1024]{1,0:T(8,128)(2,1)} %get-tuple-element.3792) | copy-start | bytes 786436
  745.4 8.7 collective-permute-start.18
  746.7 10.2 collective-permute-start.19
  797.0 16.3 %copy-start.95 = (bf16[1,128,1024]{2,1,0:T(8,128)(2,1)}, bf16[1,128,1024]{2,1,0:T(8,128)(2,1)S(1)}, u32[]{:S(2)}) copy-start(bf16[1,128,1024]{2,1,0:T(8,128)(2,1)S(1)} %get-tuple-element.3042) | copy-start | bytes 786436
  840.2 288.9 %collective-permute-start.22 = (bf16[1,1024,2816]{2,1,0:T(8,128)(2,1)}, bf16[1,1024,2816]{2,1,0:T(8,128)(2,1)}, u32[]{:S(2)}, u32[]{:S(2)}) collective-permute-start(bf16[1,1024,2816]{2,1,0:T(8,128)(2,1)} %fusion.407), channel_id=1, source_target_pairs={{0,8},{8,0},{16,24},{24,16},{1,9},{9,1},{17,25},{25,17},{2,10},{10... | collective-permute-start | bytes 17301512 | tf_op jit(solution)/shard_map/ppermute | solution.py:16
  844.9 272.5 %collective-permute-start.23 = (bf16[1,1408,1024]{2,1,0:T(8,128)(2,1)}, bf16[1,1408,1024]{2,1,0:T(8,128)(2,1)}, u32[]{:S(2)}, u32[]{:S(2)}) collective-permute-start(bf16[1,1408,1024]{2,1,0:T(8,128)(2,1)} %dynamic-slice_convert_fusion), channel_id=1, source_target_pairs={{0,8},{8,0},{16,24},{24,16},{1,9},{9,1},{17,25},{25,17},{2,10},{10... | collective-permute-start | bytes 8650760 | tf_op jit(solution)/shard_map/ppermute | solution.py:16
  866.2 257.6 %collective-permute-start.20 = (bf16[1,1024,1536]{2,1,0:T(8,128)(2,1)}, bf16[1,1024,1536]{2,1,0:T(8,128)(2,1)}, u32[]{:S(2)}, u32[]{:S(2)}) collective-permute-start(bf16[1,1024,1536]{2,1,0:T(8,128)(2,1)} %fusion.412), channel_id=1, source_target_pairs={{0,8},{8,0},{16,24},{24,16},{1,9},{9,1},{17,25},{25,17},{2,10},{10... | collective-permute-start | bytes 9437192 | tf_op jit(solution)/shard_map/ppermute | solution.py:16
  871.5 242.9 %collective-permute-start.21 = (bf16[1,512,1024]{2,1,0:T(8,128)(2,1)}, bf16[1,512,1024]{2,1,0:T(8,128)(2,1)S(1)}, u32[]{:S(2)}, u32[]{:S(2)}) collective-permute-start(bf16[1,512,1024]{2,1,0:T(8,128)(2,1)} %dynamic-slice_convert_fusion.1), channel_id=1, source_target_pairs={{0,8},{8,0},{16,24},{24,16},{1,9},{9,1},{17,25},{25,17},{2,10},{10... | collective-permute-start | bytes 3145736 | tf_op jit(solution)/shard_map/ppermute | solution.py:16
  880.1 521.4 %all-reduce.4.cloned.1.call-start = ((), (), s32[]{:S(2)}) async-start(), calls=%async_computation.4 | async-start | bytes 25690112 | tf_op jit(solution)/shard_map/psum | solution.py:478
  1138.8 278.5 %reduce-scatter.3.cloned.1.call-start = ((), (), s32[]{:S(2)}) async-start(), calls=%async_computation.2 | async-start | bytes 655360 | tf_op jit(solution)/shard_map/reduce_scatter | solution.py:434
  (67 other events, 258.2 us)
Sparse Core Ops, SparseCore 0:
  880.2 27.0 reduce-scatter.4
  1148.4 25.6 reduce-scatter.2
Sparse Core Ops, SparseCore 1:
  1138.9 262.6 all-reduce.3
where the time goes:
time: 1440 us; the launch traced here: 1430 us
  waiting for transfers between devices  531 us (37%)
  blocking collectives  350 us (24%)
  other arithmetic  225 us (16%)
  local copies, waits for them, and re-layouts  142 us (10%)
  matrix products  68.9 us (5%)
  loops' own time  50.2 us (3%)
  starting transfers between devices  38 us (3%)
  between operations  22.1 us (2%)
    all_gather x1, blocking collectives, body(): lax.all_gather(tokens, 'section', axis=1, tiled=True)  280 us
    ppermute x8, waiting for transfers between devices, partner_2(): return lax.ppermute(value, axis, pairs)  234 us
    psum x1, waiting for transfers between devices, body(): lax.psum((owned[0] + got[0]).astype(jnp.bfloat16), 'dp').astype(jnp.float32)  190 us
    ppermute x16, waiting for transfers between devices, shifted(): return lax.ppermute(x, axis, pairs)  107 us
    scatter x35, other arithmetic, body(): buf.at[slot_place].set(part)  74.7 us
    another operation x53, local copies, waits for them, and re-layouts  41.8 us
    psum x1, blocking collectives, body(): lax.psum((value_part, blend_part), ('section', 'dp'))  41.2 us
    dot_general x4, matrix products, contract_rows(): lax.dot_general(left, right, (((0,), (0,)), ((), ())), preferred_element_...  32.1 us
  transfers between devices with their start and end apart: 27, of which 10 were waited for; matrix products, arithmetic and copies ran while one was open for 13% of the time, Pallas kernels for 0%

commit v1 on v0

v1 whole, which is shorter than its diff:
```python
import functools

import jax
import jax.numpy as jnp
from jax import lax
from jax.experimental import pallas as pl
from jax.experimental.pallas import tpu as pltpu
from jax.sharding import PartitionSpec as P

HEAD_DIM = 64
EPS = 1e-05
NEG = -1e30
GROUP = 8
BF = jnp.bfloat16
F32 = jnp.float32
MIB = 1024 * 1024


def dot_nn(left, right):
    return lax.dot_general(left, right, (((1,), (0,)), ((), ())), preferred_element_type=F32)


def dot_nt(left, right):
    return lax.dot_general(left, right, (((1,), (1,)), ((), ())), preferred_element_type=F32)


def dot_tn(left, right):
    return lax.dot_general(left, right, (((0,), (0,)), ((), ())), preferred_element_type=F32)


def full(memory=pltpu.VMEM):
    return pl.BlockSpec(memory_space=memory)


def shape_of(shape, dtype):
    return jax.ShapeDtypeStruct(shape, dtype)


def normalize(stream, axis):
    rscale = lax.rsqrt(jnp.mean(stream * stream, axis=axis, keepdims=True) + EPS)
    return stream * rscale, rscale


def norm_back(stream, grad_out, dact, gain):
    normed, rscale = normalize(stream, -1)
    scaled = dact * normed
    dnorm = dact * gain
    mean = jnp.mean(scaled * gain, axis=-1, keepdims=True)
    grad = grad_out + rscale * (dnorm - normed * mean)
    return grad, jnp.sum(scaled, axis=0, keepdims=True)


def allowed_keys(ends, count):
    key = lax.broadcasted_iota(jnp.int32, (count, count), 0)
    query = lax.broadcasted_iota(jnp.int32, (count, count), 1)
    segment_key = sum((key >= end).astype(jnp.int32) for end in ends)
    segment_query = sum((query >= end).astype(jnp.int32) for end in ends)
    return (key <= query) & (segment_key == segment_query)


def head_probs(query, keys, allowed):
    scores = jnp.where(allowed, dot_tn(keys, query) * HEAD_DIM**-0.5, NEG)
    exponent = jnp.exp(scores - jnp.max(scores, axis=0, keepdims=True))
    return exponent / jnp.sum(exponent, axis=0, keepdims=True)


def head_back(query, keys, mixed, dattn, probs):
    low_probs = probs.astype(BF)
    dprobs = dot_tn(mixed, dattn)
    dscores = probs * (dprobs - jnp.sum(dprobs * probs, axis=0, keepdims=True))
    dscores = dscores.astype(BF)
    dquery = dot_nn(keys, dscores) * HEAD_DIM**-0.5
    dkeys = dot_nt(query, dscores) * HEAD_DIM**-0.5
    dmixed = dot_nt(dattn, low_probs)
    return dquery, dkeys, dmixed


def swish(gate, up):
    sigmoid = 1.0 / (1.0 + jnp.exp(-gate))
    return sigmoid, gate * sigmoid


def feed_back(gate, up, dhid):
    sigmoid, silu = swish(gate, up)
    hid = (silu * up).astype(BF)
    dgate = dhid * up * (sigmoid * (1.0 + gate * (1.0 - sigmoid)))
    dup = dhid * silu
    return hid, dgate.astype(BF), dup.astype(BF)


def attn_forward_kernel(mixing, slot, *refs):
    if mixing:
        ends_ref, x_ref, gain_ref, inward_ref, outward_ref, mix_ref, first_ref = refs[:7]
        part_ref, mixed_ref, square_ref = refs[7:]
    else:
        ends_ref, x_ref, gain_ref, inward_ref, outward_ref = refs[:5]
        part_ref, mixed_ref, square_ref = refs[5:]
    count = x_ref.shape[0]
    width = outward_ref.shape[0]
    normed, unused = normalize(x_ref[...].astype(F32), -1)
    act = (normed * gain_ref[...]).astype(BF)
    proj = dot_nn(act, inward_ref[...])
    proj = proj.T.astype(BF)
    values = proj[2 * width :]
    if mixing:
        mix = mix_ref[...]
        mixed = (1.0 - mix) * values.astype(F32) + mix * first_ref[...].astype(F32)
        values = mixed.astype(BF)
    mixed_ref[...] = values
    wide = values.astype(F32)
    square_ref[...] = jnp.sum(wide * wide, axis=0, keepdims=True)
    allowed = allowed_keys([ends_ref[slot, i] for i in range(ends_ref.shape[1])], count)
    heads = []
    for at in range(0, width, HEAD_DIM):
        probs = head_probs(proj[at : at + HEAD_DIM], proj[width + at : width + at + HEAD_DIM], allowed)
        heads.append(dot_nn(values[at : at + HEAD_DIM], probs.astype(BF)))
    attn = jnp.concatenate(heads, axis=0).T.astype(BF)
    part_ref[...] = dot_nn(attn, outward_ref[...]).astype(BF)


def feed_forward_kernel(x_ref, own_ref, got_ref, gain_ref, inward_ref, outward_ref, stream_ref, turned_ref, part_ref):
    stream = x_ref[...].astype(F32) + (own_ref[...].astype(F32) + got_ref[...].astype(F32))
    low = stream.astype(BF)
    stream_ref[...] = low
    stream = low.astype(F32)
    turned_ref[...] = stream.T.astype(BF)
    normed, unused = normalize(stream, -1)
    act = (normed * gain_ref[...]).astype(BF)
    hidden = outward_ref.shape[0]
    gate = dot_nn(act, inward_ref[:, :hidden])
    up = dot_nn(act, inward_ref[:, hidden:])
    unused, silu = swish(gate, up)
    hid = (silu * up).astype(BF)
    part_ref[...] = dot_nn(hid, outward_ref[...]).astype(BF)


def feed_backward_kernel(x_ref, grad_ref, gain_ref, inward_ref, outward_ref, part_ref):
    normed, unused = normalize(x_ref[...].astype(F32), -1)
    act = (normed * gain_ref[...]).astype(BF)
    hidden = outward_ref.shape[0]
    gate = dot_nn(act, inward_ref[:, :hidden])
    up = dot_nn(act, inward_ref[:, hidden:])
    dhid = dot_nt(grad_ref[...], outward_ref[...])
    unused, dgate, dup = feed_back(gate, up, dhid)
    dact = dot_nt(dgate, inward_ref[:, :hidden]) + dot_nt(dup, inward_ref[:, hidden:])
    part_ref[...] = dact.astype(BF)


def attn_backward_kernel(mixing, slot, *refs):
    (
        ends_ref,
        next_ref,
        grad_next_ref,
        own_ref,
        got_ref,
        gain_next_ref,
        x_ref,
        gain_ref,
        inward_ref,
        outward_ref,
        mix_ref,
        first_ref,
    ) = refs[:12]
    grad_ref, turned_ref, dgain_ref, part_ref, dfirst_ref = refs[12:]
    count = x_ref.shape[0]
    width = outward_ref.shape[0]
    dact_next = own_ref[...].astype(F32) + got_ref[...].astype(F32)
    grad, dgain = norm_back(
        next_ref[...].astype(F32), grad_next_ref[...].astype(F32), dact_next, gain_next_ref[...]
    )
    dgain_ref[...] = dgain
    low_grad = grad.astype(BF)
    grad_ref[...] = low_grad
    turned_ref[...] = low_grad.astype(F32).T.astype(BF)
    dattn = dot_nt(low_grad, outward_ref[...]).T.astype(BF)
    normed, unused = normalize(x_ref[...].astype(F32), -1)
    act = (normed * gain_ref[...]).astype(BF)
    proj = dot_nn(act, inward_ref[...]).T.astype(BF)
    values = proj[2 * width :]
    if mixing:
        mix = mix_ref[...]
        values = ((1.0 - mix) * values.astype(F32) + mix * first_ref[...].astype(F32)).astype(BF)
    allowed = allowed_keys([ends_ref[slot, i] for i in range(ends_ref.shape[1])], count)
    dquery, dkeys, dmixed = [], [], []
    for at in range(0, width, HEAD_DIM):
        query, keys = proj[at : at + HEAD_DIM], proj[width + at : width + at + HEAD_DIM]
        probs = head_probs(query, keys, allowed)
        got = head_back(query, keys, values[at : at + HEAD_DIM], dattn[at : at + HEAD_DIM], probs)
        dquery.append(got[0])
        dkeys.append(got[1])
        dmixed.append(got[2])
    dmixed = jnp.concatenate(dmixed, axis=0)
    if mixing:
        dfirst_ref[...] = (mix_ref[...] * dmixed).astype(BF)
        dvalues = (1.0 - mix_ref[...]) * dmixed
    else:
        dfirst_ref[...] = jnp.zeros_like(dfirst_ref)
        dvalues = dmixed + first_ref[...].astype(F32)
    dproj = jnp.concatenate(dquery + dkeys + [dvalues], axis=0).T.astype(BF)
    part_ref[...] = dot_nt(dproj, inward_ref[...]).astype(BF)


def combine_kernel(x_ref, grad_ref, own_ref, got_ref, gain_ref, out_ref, dgain_ref):
    dact = own_ref[...].astype(F32) + got_ref[...].astype(F32)
    grad, dgain = norm_back(x_ref[...].astype(F32), grad_ref[...].astype(F32), dact, gain_ref[...])
    out_ref[...] = grad.astype(out_ref.dtype)
    dgain_ref[...] = dgain


def call(kernel, outs, *args, smem=0, flops=0, name=None):
    moved = sum(a.size * a.dtype.itemsize for a in args) + sum(o.size * o.dtype.itemsize for o in outs)
    return pl.pallas_call(
        kernel,
        out_shape=outs,
        in_specs=[full(pltpu.SMEM)] * smem + [full()] * (len(args) - smem),
        out_specs=[full()] * len(outs),
        compiler_params=pltpu.CompilerParams(vmem_limit_bytes=40 * MIB),
        cost_estimate=pl.CostEstimate(flops=int(flops), bytes_accessed=int(moved), transcendentals=0),
        name=name,
    )(*args)


def fetch(pick, choices, target, sems, first):
    count = choices[0].shape[2]
    for which, source in enumerate(choices):

        @pl.when(pick == which)
        def _():
            for slot in range(source.shape[0]):
                pltpu.make_async_copy(
                    source.at[slot], target.at[:, slot * count : (slot + 1) * count], sems.at[first + slot]
                ).start()


def arrived(choices, target, sems, first, slots):
    count = choices[0].shape[2]
    for slot in slots:
        pltpu.make_async_copy(
            choices[0].at[0], target.at[:, pl.ds(slot * count, count)], sems.at[first + slot]
        ).wait()


def feed_weights_kernel(
    steps,
    slots,
    pick_ref,
    s0_ref,
    s1_ref,
    g0_ref,
    g1_ref,
    gain_ref,
    inward_ref,
    outward_ref,
    dinward_ref,
    doutward_ref,
    stream,
    grad,
    hid_all,
    dboth_all,
    sems,
):
    step = pl.program_id(0)
    count = s0_ref.shape[2]
    hidden = outward_ref.shape[0]
    rows, wide, across = steps

    @pl.when(step == 0)
    def _():
        fetch(pick_ref[0], (s0_ref, s1_ref), stream, sems, 0)
        fetch(pick_ref[0], (g0_ref, g1_ref), grad, sems, slots)

    @pl.when(step < rows)
    def _():
        each = slots // rows
        mine = [step * each + i for i in range(each)]
        arrived((s0_ref,), stream, sems, 0, mine)
        arrived((g0_ref,), grad, sems, slots, mine)
        here = pl.ds(pl.multiple_of(step * (each * count), each * count), each * count)
        normed, unused = normalize(stream[:, here].astype(F32), 0)
        act = (normed * gain_ref[...]).astype(BF)
        stream[:, here] = act
        both = dot_nn(inward_ref[...], act)
        dhid = dot_nn(outward_ref[...], grad[:, here])
        hid, dgate, dup = feed_back(both[:hidden], both[hidden:], dhid)
        hid_all[:, here] = hid
        dboth_all[:hidden, here] = dgate
        dboth_all[hidden:, here] = dup

    @pl.when((step >= rows) & (step < rows + wide))
    def _():
        size = dinward_ref.shape[1]
        at = pl.multiple_of((step - rows) * size, size)
        dinward_ref[...] = dot_nt(stream[...], dboth_all[pl.ds(at, size), :])

    @pl.when(step >= rows + wide)
    def _():
        size = doutward_ref.shape[1]
        at = pl.multiple_of((step - rows - wide) * size, size)
        doutward_ref[...] = dot_nt(hid_all[...], grad[pl.ds(at, size), :])


def attn_weights_kernel(
    steps,
    slots,
    pick_ref,
    ends_ref,
    s0_ref,
    s1_ref,
    g0_ref,
    g1_ref,
    first_ref,
    gain_ref,
    mix_ref,
    add_ref,
    inward_ref,
    outward_ref,
    dinward_ref,
    doutward_ref,
    stream,
    grad,
    attn_all,
    dproj_all,
    sems,
):
    step = pl.program_id(0)
    count = s0_ref.shape[2]
    width = outward_ref.shape[0]
    rows, wide, across = steps

    @pl.when(step == 0)
    def _():
        fetch(pick_ref[0], (s0_ref, s1_ref), stream, sems, 0)
        fetch(pick_ref[0], (g0_ref, g1_ref), grad, sems, slots)

    @pl.when(step < rows)
    def _():
        each = slots // rows
        mine = [step * each + i for i in range(each)]
        arrived((s0_ref,), stream, sems, 0, mine)
        arrived((g0_ref,), grad, sems, slots, mine)
        here = pl.ds(pl.multiple_of(step * (each * count), each * count), each * count)
        normed, unused = normalize(stream[:, here].astype(F32), 0)
        act = (normed * gain_ref[...]).astype(BF)
        stream[:, here] = act
        proj = dot_nn(inward_ref[...], act).astype(BF)
        dattn = dot_nn(outward_ref[...], grad[:, here]).astype(BF)
        mix = mix_ref[...]
        for i in range(each):
            cols = slice(i * count, (i + 1) * count)
            place = pl.ds(pl.multiple_of((step * each + i) * count, count), count)
            first = first_ref[i].astype(F32)
            values = proj[2 * width :, cols].astype(F32)
            values = ((1.0 - mix) * values + mix * first).astype(BF)
            allowed = allowed_keys([ends_ref[step * each + i, j] for j in range(ends_ref.shape[1])], count)
            for at in range(0, width, HEAD_DIM):
                query, keys = proj[at : at + HEAD_DIM, cols], proj[width + at : width + at + HEAD_DIM, cols]
                probs = head_probs(query, keys, allowed)
                head = slice(at, at + HEAD_DIM)
                attn_all[head, place] = dot_nn(values[head], probs.astype(BF)).astype(BF)
                dquery, dkeys, dmixed = head_back(query, keys, values[head], dattn[head, cols], probs)
                dproj_all[at : at + HEAD_DIM, place] = dquery.astype(BF)
                dproj_all[width + at : width + at + HEAD_DIM, place] = dkeys.astype(BF)
                dvalues = (1.0 - mix[head]) * dmixed + add_ref[head, :] * first[head]
                dproj_all[2 * width + at : 2 * width + at + HEAD_DIM, place] = dvalues.astype(BF)

    @pl.when((step >= rows) & (step < rows + wide))
    def _():
        size = dinward_ref.shape[1]
        at = pl.multiple_of((step - rows) * size, size)
        dinward_ref[...] = dot_nt(stream[...], dproj_all[pl.ds(at, size), :])

    @pl.when(step >= rows + wide)
    def _():
        size = doutward_ref.shape[1]
        at = pl.multiple_of((step - rows - wide) * size, size)
        doutward_ref[...] = dot_nt(attn_all[...], grad[pl.ds(at, size), :])


def weight_call(kernel, smem, gathered, extra, small, weights, name):
    slots, model, count = gathered[0].shape
    inward, outward = weights
    total = slots * count
    each = 2
    block = 256
    rows, wide, across = slots // each, inward.shape[0] // block, model // block
    steps = (rows, wide, across)
    once = dict(pipeline_mode=pl.Buffered(1))

    def whole(a):
        return pl.BlockSpec(a.shape, lambda i: (0,) * a.ndim, **once)

    in_specs = (
        [full(pltpu.SMEM)] * len(smem)
        + [full(pl.ANY)] * 4
        + [pl.BlockSpec((each,) + a.shape[1:], lambda i: (jnp.minimum(i, rows - 1), 0, 0)) for a in extra]
        + [whole(a) for a in small]
        + [whole(a) for a in weights]
    )
    out_specs = [
        pl.BlockSpec((model, block), lambda i: (0, jnp.clip(i - rows, 0, wide - 1))),
        pl.BlockSpec((outward.shape[0], block), lambda i: (0, jnp.clip(i - rows - wide, 0, across - 1))),
    ]
    flops = 4 * total * (inward.size + outward.size)
    return pl.pallas_call(
        functools.partial(kernel, steps, slots),
        grid=(rows + wide + across,),
        in_specs=in_specs,
        out_specs=out_specs,
        out_shape=[
            shape_of((model, inward.shape[0]), F32),
            shape_of((outward.shape[0], model), F32),
        ],
        scratch_shapes=[
            pltpu.VMEM((model, total), BF),
            pltpu.VMEM((model, total), BF),
            pltpu.VMEM((outward.shape[0], total), BF),
            pltpu.VMEM((inward.shape[0], total), BF),
            pltpu.SemaphoreType.DMA((2 * slots,)),
        ],
        compiler_params=pltpu.CompilerParams(
            vmem_limit_bytes=60 * MIB, dimension_semantics=("arbitrary",)
        ),
        cost_estimate=pl.CostEstimate(flops=flops, bytes_accessed=16 * MIB, transcendentals=0),
        name=name,
    )(*smem, *gathered, *extra, *small, *weights)


def section_pairs(mask):
    return [(i, i ^ mask) for i in range(lax.axis_size("section"))]


def body(tokens, cotangent, gains, attn_in, attn_out, ffn_in, ffn_out, mix_level, seq_lengths):
    section = lax.axis_index("section")
    lower = section < 2
    even = section % 2 == 0
    dp = lax.axis_size("dp")
    group = min(dp, GROUP)
    groups = [list(range(at, at + group)) for at in range(0, dp, group)]
    micro = seq_lengths.shape[0]
    count = tokens.shape[0] // micro
    piece = tokens.shape[1]
    inward, outward, feed_in, feed_out = attn_in[0], attn_out[0], ffn_in[0], ffn_out[0]
    model = inward.shape[0]
    width = outward.shape[0]
    hidden = feed_out.shape[0]

    def swap(x, mask):
        return lax.ppermute(x, "section", section_pairs(mask))

    def to_upper(x):
        return lax.ppermute(x, "section", [(0, 2), (1, 3)])

    def to_lower(x):
        return lax.ppermute(x, "section", [(2, 0), (3, 1)])

    def gathered(parts):
        return lax.all_gather(jnp.stack(parts), "dp", axis=0, tiled=True, axis_index_groups=groups)

    near = jnp.where(lower, tokens, cotangent)
    far = jnp.where(lower, cotangent, tokens)
    got_near, got_far, got_across = swap(near, 1), swap(far, 2), swap(far, 3)
    ours = [jnp.where(even, near, got_near), jnp.where(even, got_near, near)]
    theirs = [jnp.where(even, got_far, got_across), jnp.where(even, got_across, got_far)]
    given = jnp.concatenate(
        [jnp.where(lower, a, b) for a, b in zip(ours + theirs, theirs + ours)], axis=1
    )
    given = [given[m * count : (m + 1) * count] for m in range(micro)]

    got_gains = swap(gains, 1)
    gain_attn = jnp.where(even, gains, got_gains)
    gain_feed = jnp.where(even, got_gains, gains)
    ends = jnp.cumsum(seq_lengths, axis=1)
    all_ends = lax.all_gather(ends, "dp", axis=0, tiled=True, axis_index_groups=groups)
    mix_all = jnp.repeat(mix_level.astype(F32) / 8.0, HEAD_DIM)
    mix = jnp.where(even, mix_all[:width], mix_all[width:])[:, None]

    inward_turned = inward.T
    feed_in_turned = feed_in.T

    all_given = gathered([x.T for x in given])

    attn_flops = 2 * count * (inward.size + outward.size)
    feed_flops = 2 * count * (feed_in.size + feed_out.size)
    low_stream = shape_of((count, model), BF)
    low_values = shape_of((width, count), BF)
    turned_shape = shape_of((model, count), BF)
    row_sum = shape_of((1, model), F32)

    def attn_forward(slot, x, first):
        args = (ends, x, gain_attn, inward, outward)
        if first is not None:
            args += (mix, first)
        return call(
            functools.partial(attn_forward_kernel, first is not None, slot),
            [low_stream, low_values, shape_of((1, count), F32)],
            *args,
            smem=1,
            flops=attn_flops,
            name="attn_forward",
        )

    def feed_forward(x, own, got):
        return call(
            feed_forward_kernel,
            [low_stream, turned_shape, low_stream],
            x,
            own,
            got,
            gain_feed,
            feed_in,
            feed_out,
            flops=feed_flops,
            name="feed_forward",
        )

    def feed_backward(x, grad):
        return call(
            feed_backward_kernel,
            [low_stream],
            x,
            grad,
            gain_feed,
            feed_in,
            feed_out,
            flops=2 * feed_flops,
            name="feed_backward",
        )[0]

    def attn_backward(mixing, slot, x_next, grad_next, own, got, x, first):
        return call(
            functools.partial(attn_backward_kernel, mixing, slot),
            [low_stream, turned_shape, row_sum, low_stream, low_values],
            ends,
            x_next,
            grad_next,
            own,
            got,
            gain_feed,
            x,
            gain_attn,
            inward,
            outward,
            mix,
            first,
            smem=1,
            flops=2 * attn_flops,
            name="attn_backward",
        )

    def combine(x, grad, own, got, dtype):
        return call(
            combine_kernel,
            [shape_of((count, model), dtype), row_sum],
            x,
            grad,
            own,
            got,
            gain_attn,
            flops=1000,
            name="combine",
        )

    def forward_layer(xs, firsts):
        parts, mixed, squares = zip(*[attn_forward(m, xs[m], firsts[m]) for m in range(micro)])
        streams, turned, fparts = [], [], []
        for m in range(micro):
            a, b, c = feed_forward(xs[m], parts[m], swap(parts[m], 1))
            streams.append(a)
            turned.append(b)
            fparts.append(c)
        outs = []
        for m in range(micro):
            got = swap(fparts[m], 1)
            outs.append(
                (streams[m].astype(F32) + (fparts[m].astype(F32) + got.astype(F32))).astype(BF)
            )
        return streams, turned, outs, mixed, sum(jnp.sum(s) for s in squares)

    def backward_layer(mixing, mids, xs, grads, firsts, dtype):
        own = [feed_backward(mids[m], grads[m]) for m in range(micro)]
        results = [
            attn_backward(mixing, m, mids[m], grads[m], own[m], swap(own[m], 1), xs[m], firsts[m])
            for m in range(micro)
        ]
        outs = [
            combine(xs[m], results[m][0], results[m][3], swap(results[m][3], 1), dtype)
            for m in range(micro)
        ]
        dgain_feed = sum(r[2] for r in results)
        dgain_attn = sum(o[1] for o in outs)
        turned = [r[1] for r in results]
        dfirst = [r[4] for r in results]
        return [o[0] for o in outs], turned, dfirst, dgain_attn, dgain_feed

    mid0, mid0_turned, out0, first0, square0 = forward_layer(given, [None] * micro)
    first1 = [to_upper(v) for v in first0]
    x1 = [to_upper(x) for x in out0]
    all_second = gathered([jnp.where(lower, a, b.T) for a, b in zip(mid0_turned, x1)])
    mid1, mid1_turned, out1, unused, square1 = forward_layer(x1, first1)
    all_third = gathered(mid1_turned)

    grads1, turned1, dfirst1, dgain_attn1, dgain_feed1 = backward_layer(
        True, mid1, x1, given, first1, BF
    )
    dfirst0 = [to_lower(v) for v in dfirst1]
    grads_in = [to_lower(g) for g in grads1]
    all_first = gathered([jnp.where(lower, a, b) for a, b in zip(dfirst0, first1)])
    all_fourth = gathered([jnp.where(lower, a.T, b) for a, b in zip(grads_in, turned1)])
    grads0, turned0, unused, dgain_attn0, dgain_feed0 = backward_layer(
        False, mid0, given, grads_in, dfirst0, F32
    )
    all_fifth = gathered(turned0)

    pick = jnp.where(lower, 0, 1).astype(jnp.int32)[None]
    d_feed_in, d_feed_out = weight_call(
        feed_weights_kernel,
        (pick,),
        (all_second, all_third, all_fourth, all_given),
        (),
        (gain_feed.reshape(model, 1),),
        (feed_in_turned, feed_out),
        "feed_weights",
    )
    d_in, d_out = weight_call(
        attn_weights_kernel,
        (pick, all_ends),
        (all_given, all_second, all_fifth, all_fourth),
        (all_first,),
        (
            gain_attn.reshape(model, 1),
            jnp.where(lower, 0.0, mix),
            jnp.where(lower, jnp.ones_like(mix), 0.0),
        ),
        (inward_turned, outward),
        "attn_weights",
    )

    def over_groups(x):
        if dp == group:
            return x
        across = [list(range(at, dp, group)) for at in range(group)]
        return lax.psum(x.astype(BF), "dp", axis_index_groups=across).astype(F32)

    d_in, d_out, d_feed_in, d_feed_out = [
        over_groups(x)[None] for x in (d_in, d_out, d_feed_in, d_feed_out)
    ]
    dgain_attn = jnp.where(lower, dgain_attn0, dgain_attn1)
    dgain_feed = jnp.where(lower, dgain_feed0, dgain_feed1)
    d_gain = lax.psum(jnp.where(even, dgain_attn, dgain_feed), "dp")

    squares = jnp.stack([jnp.where(lower, square0, 0.0), jnp.where(lower, 0.0, square1)])
    totals = lax.psum(squares, ("section", "dp")) / (micro * count * dp * 2 * width)

    def spread(rows, own_lower):
        mine = lax.dynamic_slice_in_dim(rows, section * piece, piece, 1)
        if own_lower:
            sent = lax.dynamic_slice_in_dim(rows, ((section + 2) % 4) * piece, piece, 1)
            return jnp.where(lower, mine, to_upper(sent.astype(BF)).astype(rows.dtype))
        sent = lax.dynamic_slice_in_dim(rows, ((section + 2) % 4) * piece, piece, 1)
        return jnp.where(lower, to_lower(sent), mine)

    out = spread(jnp.concatenate(out1, axis=0), False)
    dinput = spread(jnp.concatenate(grads0, axis=0), True)
    return (out, dinput, d_gain, d_in, d_out, d_feed_in, d_feed_out, totals[0], totals[1])


def solution(mesh):
    in_specs = (
        P("dp", "section"),
        P("dp", "section"),
        P("section", None),
        P("section", None, None),
        P("section", None, None),
        P("section", None, None),
        P("section", None, None),
        P(),
        P("dp", None),
    )
    out_specs = (
        P("dp", "section"),
        P("dp", "section"),
        P("section", None),
        P("section", None, None),
        P("section", None, None),
        P("section", None, None),
        P("section", None, None),
        P(),
        P(),
    )
    return jax.shard_map(body, mesh=mesh, in_specs=in_specs, out_specs=out_specs, check_vma=False)
```

time: 1440 us -> 449 us (0.31)
  waiting for transfers between devices: 531 us -> 49.6 us
  blocking collectives: 350 us -> 65.2 us
  other arithmetic: 225 us -> 13.9 us
  Pallas kernels: 0 us -> 195 us
  local copies, waits for them, and re-layouts: 142 us -> 49.5 us
  matrix products: 68.9 us -> 0 us
  loops' own time: 50.2 us -> 0 us
    ppermute x24 -> x30, waiting for transfers between devices: 341 us -> 49.5 us  [the longest x20 32.9 us: swap(): return lax.ppermute(x, 'section', section_pairs(mask))]
    all_gather x2 -> x1, blocking collectives: 292 us -> 12.5 us  [body(): lax.all_gather(ends, 'dp', axis=0, tiled=True, axis_index_groups=groups)]
    pallas_call x0 -> x22, Pallas kernels: none -> 195 us  [the longest x2 134 us: weight_call(): pl.pallas_call(functools.partial(kernel, steps, slots), grid=(rows + wide...]
    psum x1 -> x0, waiting for transfers between devices: 190 us -> none  [body(): lax.psum((owned[0] + got[0]).astype(jnp.bfloat16), 'dp').astype(jnp.float32)]
    scatter x50 -> x0, other arithmetic: 94.1 us -> none  [the longest x35 74.7 us: body(): buf.at[slot_place].set(part)]
    dot_general x26 -> x0, matrix products: 68.9 us -> none  [the longest x4 32.1 us: contract_rows(): lax.dot_general(left, right, (((0,), (0,)), ((), ())), preferred_element_...]
    convert_element_type x20 -> x4, other arithmetic: 59.1 us -> 1.44 us  [forward_layer(): (streams[m].astype(F32) + (fparts[m].astype(F32) + got.astype(F32))).asty...]
    another operation x10 -> x0, loops' own time: 50.2 us -> none  [the longest x5 31.8 us: body(): lax.switch(branch, (resting_backward, attn_backward, feed_backward_branch...]
  transfers between devices with their start and end apart: 27 -> 36, of which waited for: 10 -> 23; matrix products, arithmetic and copies ran while one was open for 13% -> 8% of each run, Pallas kernels for 0% -> 26%
where the time goes in v1:
time: 449 us; the launch traced here: 441 us
  Pallas kernels  195 us (43%)
  blocking collectives  65.2 us (15%)
  starting transfers between devices  50 us (11%)
  waiting for transfers between devices  49.6 us (11%)
  local copies, waits for them, and re-layouts  49.5 us (11%)
  between operations  18.3 us (4%)
  other arithmetic  13.9 us (3%)
    pallas_call x2, Pallas kernels, weight_call(): pl.pallas_call(functools.partial(kernel, steps, slots), grid=(rows + wide...  134 us
    pallas_call x20, Pallas kernels, call(): pl.pallas_call(kernel, out_shape=outs, in_specs=[full(pltpu.SMEM)] * smem...  61 us
    psum x1, blocking collectives, body(): lax.psum(squares, ('section', 'dp')) / (micro * count * dp * 2 * width)  38.3 us
    unnamed x169, local copies, waits for them, and re-layouts  34.7 us
    ppermute x20, waiting for transfers between devices, swap(): return lax.ppermute(x, 'section', section_pairs(mask))  32.9 us
    ppermute x20, starting transfers between devices, swap(): return lax.ppermute(x, 'section', section_pairs(mask))  25.6 us
    ppermute x5, starting transfers between devices, to_upper(): return lax.ppermute(x, 'section', [(0, 2), (1, 3)])  17.3 us
    psum x1, blocking collectives, body(): d_gain = lax.psum(jnp.where(even, dgain_attn, dgain_feed), 'dp')  14.4 us
  transfers between devices with their start and end apart: 36, of which 23 were waited for; matrix products, arithmetic and copies ran while one was open for 8% of the time, Pallas kernels for 26%

profile of v1, /device:TPU:0, one launch (start us, length us, event | category | flops | bytes accessed | tf_op | source)
XLA Modules:
  0.0 441.5 jit_solution(9531914389792988688)
XLA Ops:
  8.3 4.0 collective-permute-start.2
  12.9 3.3 collective-permute-done.2
  27.9 3.2 attn_forward.6
  32.7 3.2 attn_forward.4
  42.7 3.1 collective-permute-done.4.got_ref
  48.3 3.1 collective-permute-done.11
  55.0 3.6 collective-permute-start.6
  60.9 2.9 collective-permute-done.6.refs_1_.x_ref.refs_6_
  65.0 4.5 %collective-permute-start.13 = (bf16[512,128]{1,0:T(8,128)(2,1)}, bf16[512,128]{1,0:T(8,128)(2,1)S(1)}, u32[]{:S(2)}, u32[]{:S(2)}) collective-permute-start(bf16[512,128]{1,0:T(8,128)(2,1)} %get-tuple-element.71), channel_id=1, source_target_pairs={{0,16},{8,24},{1,17},{9,25},{2,18},{10,26},{3,19},{11,27},{4,20},{... | collective-permute-start | bytes 393224 | tf_op jit(solution)/shard_map/ppermute | solution.py:451
  77.0 3.8 attn_forward.5
  81.6 3.3 attn_forward.7
  86.2 3.5 collective-permute-done.8.got_ref
  101.8 3.8 feed_backward.4.refs_3_
  106.3 3.8 feed_backward.6.refs_3_
  113.1 5.3 %attn_backward.4 = (bf16[128,1024]{1,0:T(8,128)(2,1)S(1)}, bf16[1024,128]{1,0:T(8,128)(2,1)S(1)}, f32[1,1024]{1,0:T(1,128)S(1)}, bf16[128,1024]{1,0:T(8,128)(2,1)S(1)}, bf16[512,128]{1,0:T(8,128)(2,1)S(1)}) custom-call(s32[2,4]{1,0:T(2,128)S(1)} %reduce_window_sum.11.refs_0_, bf16[128,1024]{1,0:T(8,128)(2,1)S(1)} %copy-done.28, ...), custom_call_target="tpu_custom_call" | custom-call | flops 1073741824 | bytes 6567968 | tf_op jit(solution)/shard_map/attn_backward/pallas_call | solution.py:212
  120.8 5.1 %attn_backward.6 = (bf16[128,1024]{1,0:T(8,128)(2,1)S(1)}, bf16[1024,128]{1,0:T(8,128)(2,1)S(1)}, f32[1,1024]{1,0:T(1,128)S(1)}, bf16[128,1024]{1,0:T(8,128)(2,1)S(1)}, bf16[512,128]{1,0:T(8,128)(2,1)S(1)}) custom-call(s32[2,4]{1,0:T(2,128)S(1)} %reduce_window_sum.11.refs_0_, bf16[128,1024]{1,0:T(8,128)(2,1)S(1)} %copy-done.31, ...), custom_call_target="tpu_custom_call" | custom-call | flops 1073741824 | bytes 6567968 | tf_op jit(solution)/shard_map/attn_backward/pallas_call | solution.py:212
  149.3 4.5 %collective-permute-done.21.refs_11_ = bf16[512,128]{1,0:T(8,128)(2,1)S(1)} collective-permute-done((bf16[512,128]{1,0:T(8,128)(2,1)}, bf16[512,128]{1,0:T(8,128)(2,1)S(1)}, u32[]{:S(2)}, u32[]{:S(2)}) %collective-permute-start.21) | collective-permute-done | bytes 131104 | tf_op jit(solution)/shard_map/ppermute | solution.py:454
  162.1 4.8 %feed_backward.5.refs_3_ = bf16[128,1024]{1,0:T(8,128)(2,1)S(1)} custom-call(bf16[128,1024]{1,0:T(8,128)(2,1)S(1)} %copy-done.34, bf16[128,1024]{1,0:T(8,128)(2,1)} %collective-permute-done.19.grad_ref.refs_2_, f32[1,1024]{1,0:T(1,128)S(1)} %get-tuple-element.141.gain_ref.refs_5_, bf16[1024,2816]{1,0:T(8,128)(2,1)S(1)} %bitcast.73, ...), custom_call_target="tpu_custom_call" | custom-call | flops 2214592512 | bytes 9441280 | tf_op jit(solution)/shard_map/feed_backward/pallas_call | solution.py:212
  169.5 4.8 %feed_backward.7.refs_3_ = bf16[128,1024]{1,0:T(8,128)(2,1)S(1)} custom-call(bf16[128,1024]{1,0:T(8,128)(2,1)S(1)} %copy-done.26, bf16[128,1024]{1,0:T(8,128)(2,1)} %collective-permute-done.25.grad_ref.refs_2_, f32[1,1024]{1,0:T(1,128)S(1)} %get-tuple-element.141.gain_ref.refs_5_, bf16[1024,2816]{1,0:T(8,128)(2,1)S(1)} %bitcast.74, ...), custom_call_target="tpu_custom_call" | custom-call | flops 2214592512 | bytes 9441280 | tf_op jit(solution)/shard_map/feed_backward/pallas_call | solution.py:212
  175.7 5.3 %attn_backward.5 = (bf16[128,1024]{1,0:T(8,128)(2,1)S(1)}, bf16[1024,128]{1,0:T(8,128)(2,1)S(1)}, f32[1,1024]{1,0:T(1,128)S(1)}, bf16[128,1024]{1,0:T(8,128)(2,1)S(1)}, bf16[512,128]{1,0:T(8,128)(2,1)}) custom-call(s32[2,4]{1,0:T(2,128)S(1)} %reduce_window_sum.11.refs_0_, bf16[128,1024]{1,0:T(8,128)(2,1)S(1)} %copy-done.34, ...), custom_call_target="tpu_custom_call" | custom-call | flops 1073741824 | bytes 6567968 | tf_op jit(solution)/shard_map/attn_backward/pallas_call | solution.py:212
  181.7 5.4 %attn_backward.7 = (bf16[128,1024]{1,0:T(8,128)(2,1)S(1)}, bf16[1024,128]{1,0:T(8,128)(2,1)S(1)}, f32[1,1024]{1,0:T(1,128)S(1)}, bf16[128,1024]{1,0:T(8,128)(2,1)S(1)}, bf16[512,128]{1,0:T(8,128)(2,1)}) custom-call(s32[2,4]{1,0:T(2,128)S(1)} %reduce_window_sum.11.refs_0_, bf16[128,1024]{1,0:T(8,128)(2,1)S(1)} %copy-done.26, ...), custom_call_target="tpu_custom_call" | custom-call | flops 1073741824 | bytes 6567968 | tf_op jit(solution)/shard_map/attn_backward/pallas_call | solution.py:212
  190.1 3.2 copy.155
  193.3 8.5 %copy.157 = bf16[1,1024,2816]{1,2,0:T(8,128)(2,1)} copy(bf16[1,1024,2816]{2,1,0:T(8,128)(2,1)} %param.14) | data formatting | bytes 11534336 | tf_op args[5]
  201.8 12.5 %all-gather = s32[8,2,4]{2,1,0:T(2,128)} all-gather(s32[1,2,4]{2,1,0:T(2,128)S(1)} %bitcast.107), channel_id=1, replica_groups={{0,1,2,3,4,5,6,7},{8,9,10,11,12,13,14,15},{16,17,18,19,20,21,22,23},{24..., dimensions={0}, use_global_device_ids=true | all-gather | bytes 288 | tf_op jit(solution)/shard_map/all_gather | solution.py:473
  224.7 38.3 %psum.15 = f32[2]{0:T(128)S(1)} all-reduce(f32[2]{0:T(128)S(1)} %pad_maximum_fusion.7), channel_id=1, replica_groups=mesh['section'=4,'dp'=8] {'section','dp'}, use_global_device_ids=true, to_apply=%region_6.7 | all-reduce | flops 2 | bytes 16 | tf_op jit(solution)/shard_map/psum | solution.py:652
  268.7 2.8 collective-permute-done.16
  272.2 3.0 collective-permute-done.22.got_ref
  275.5 3.9 collective-permute-done.28.got_ref
  279.9 4.3 collective-permute-start.29
  284.2 14.4 %psum.14 = f32[1,1024]{1,0:T(1,128)} all-reduce(f32[1,1024]{1,0:T(1,128)S(1)} %broadcast_select_fusion.13), channel_id=1, replica_groups=mesh['section'=4,'dp'=8] {'dp'}, use_global_device_ids=true, to_apply=%region_1.2 | all-reduce | flops 1024 | bytes 8192 | tf_op jit(solution)/shard_map/psum | solution.py:649
  299.4 53.1 %feed_weights.1 = (f32[1024,2816]{1,0:T(8,128)}, f32[1408,1024]{1,0:T(8,128)}) custom-call(s32[1]{0:T(128)} %bitcast.6.pick_ref, bf16[16,1024,128]{2,1,0:T(8,128)(2,1)} %all-gather.10.cloned.1.call-done.s1_ref.s0_ref, bf16[16,1024,128]{2,1,0:T(8,128)(2,1)} %all-gather.18.cloned.1.call-done.s1_ref, ...), custom_call_target="tpu_custom_call" | custom-call | flops 35433480192 | bytes 16777216 | tf_op jit(solution)/shard_map/feed_weights/pallas_call | solution.py:404
  353.2 81.0 %attn_weights.1 = (f32[1024,1536]{1,0:T(8,128)}, f32[512,1024]{1,0:T(8,128)}) custom-call(s32[1]{0:T(128)} %bitcast.6.pick_ref, s32[16,4]{1,0:T(8,128)} %bitcast.110, bf16[16,1024,128]{2,1,0:T(8,128)(2,1)} %all-gather.8.cloned.1.call-done.s0_ref.g1_ref, bf16[16,1024,128]{2,1,0:T(8,128)(2,1)} %all-gather.10.cloned.1.call-done.s1_ref.s0_ref, ...), custom_call_target="tpu_custom_call" | custom-call | flops 17179869184 | bytes 16777216 | tf_op jit(solution)/shard_map/attn_weights/pallas_call | solution.py:404
  (292 shorter events, 113.9 us)
Async XLA Ops:
  7.2 292.1 %all-gather.8.cloned.1.call-start = ((), (), s32[]{:S(2)}) async-start(), calls=%async_computation | async-start | bytes 4718592 | tf_op jit(solution)/shard_map/all_gather | solution.py:457
  8.3 7.9 %collective-permute-start.2 = (bf16[256,256]{1,0:T(8,128)(2,1)S(1)}, bf16[256,256]{1,0:T(8,128)(2,1)S(1)}, u32[]{:S(2)}, u32[]{:S(2)}) collective-permute-start(bf16[256,256]{1,0:T(8,128)(2,1)S(1)} %get-tuple-element.139), channel_id=1, source_target_pairs={{0,24},{8,16},{16,8},{24,0},{1,25},{9,17},{17,9},{25,1},{2,26},{10... | collective-permute-start | bytes 393224 | tf_op jit(solution)/shard_map/ppermute | solution.py:448
  22.2 277.1 %all-gather.10.cloned.1.call-start = ((), (), s32[]{:S(2)}) async-start(), calls=%async_computation.1 | async-start | bytes 4718592 | tf_op jit(solution)/shard_map/all_gather | solution.py:457
  31.1 7.4 %collective-permute-start.10 = (bf16[128,1024]{1,0:T(8,128)(2,1)S(1)}, bf16[128,1024]{1,0:T(8,128)(2,1)S(1)}, u32[]{:S(2)}, u32[]{:S(2)}) collective-permute-start(bf16[128,1024]{1,0:T(8,128)(2,1)S(1)} %get-tuple-element.68.own_ref), channel_id=1, source_target_pairs={{0,8},{8,0},{16,24},{24,16},{1,9},{9,1},{17,25},{25,17},{2,10},{10... | collective-permute-start | bytes 786440 | tf_op jit(solution)/shard_map/ppermute | solution.py:448
  36.6 9.2 %collective-permute-start.4 = (bf16[128,1024]{1,0:T(8,128)(2,1)S(1)}, bf16[128,1024]{1,0:T(8,128)(2,1)S(1)}, u32[]{:S(2)}, u32[]{:S(2)}) collective-permute-start(bf16[128,1024]{1,0:T(8,128)(2,1)S(1)} %get-tuple-element.61.own_ref), channel_id=1, source_target_pairs={{0,8},{8,0},{16,24},{24,16},{1,9},{9,1},{17,25},{25,17},{2,10},{10... | collective-permute-start | bytes 786440 | tf_op jit(solution)/shard_map/ppermute | solution.py:448
  40.1 11.3 %collective-permute-start.11 = (bf16[128,1024]{1,0:T(8,128)(2,1)S(1)}, bf16[128,1024]{1,0:T(8,128)(2,1)S(1)}, u32[]{:S(2)}, u32[]{:S(2)}) collective-permute-start(bf16[128,1024]{1,0:T(8,128)(2,1)S(1)} %get-tuple-element.70), channel_id=1, source_target_pairs={{0,8},{8,0},{16,24},{24,16},{1,9},{9,1},{17,25},{25,17},{2,10},{10... | collective-permute-start | bytes 786440 | tf_op jit(solution)/shard_map/ppermute | solution.py:448
  47.4 7.4 %collective-permute-start.5 = (bf16[128,1024]{1,0:T(8,128)(2,1)S(1)}, bf16[128,1024]{1,0:T(8,128)(2,1)S(1)}, u32[]{:S(2)}, u32[]{:S(2)}) collective-permute-start(bf16[128,1024]{1,0:T(8,128)(2,1)S(1)} %get-tuple-element.63), channel_id=1, source_target_pairs={{0,8},{8,0},{16,24},{24,16},{1,9},{9,1},{17,25},{25,17},{2,10},{10... | collective-permute-start | bytes 786440 | tf_op jit(solution)/shard_map/ppermute | solution.py:448
  51.6 9.3 %collective-permute-start.12 = (bf16[128,1024]{1,0:T(8,128)(2,1)S(1)}, bf16[128,1024]{1,0:T(8,128)(2,1)S(1)}, u32[]{:S(2)}, u32[]{:S(2)}) collective-permute-start(bf16[128,1024]{1,0:T(8,128)(2,1)S(1)} %add_convert_fusion.1), channel_id=1, source_target_pairs={{0,16},{8,24},{1,17},{9,25},{2,18},{10,26},{3,19},{11,27},{4,20},{... | collective-permute-start | bytes 786440 | tf_op jit(solution)/shard_map/ppermute | solution.py:451
  55.0 8.8 %collective-permute-start.6 = (bf16[128,1024]{1,0:T(8,128)(2,1)S(1)}, bf16[128,1024]{1,0:T(8,128)(2,1)S(1)}, u32[]{:S(2)}, u32[]{:S(2)}) collective-permute-start(bf16[128,1024]{1,0:T(8,128)(2,1)S(1)} %add_convert_fusion.3), channel_id=1, source_target_pairs={{0,16},{8,24},{1,17},{9,25},{2,18},{10,26},{3,19},{11,27},{4,20},{... | collective-permute-start | bytes 786440 | tf_op jit(solution)/shard_map/ppermute | solution.py:451
  64.9 234.4 %all-gather.18.cloned.1.call-start = ((), (), s32[]{:S(2)}) async-start(), calls=%async_computation.5 | async-start | bytes 4718592 | tf_op jit(solution)/shard_map/all_gather | solution.py:457
  65.0 16.6 %collective-permute-start.13 = (bf16[512,128]{1,0:T(8,128)(2,1)}, bf16[512,128]{1,0:T(8,128)(2,1)S(1)}, u32[]{:S(2)}, u32[]{:S(2)}) collective-permute-start(bf16[512,128]{1,0:T(8,128)(2,1)} %get-tuple-element.71), channel_id=1, source_target_pairs={{0,16},{8,24},{1,17},{9,25},{2,18},{10,26},{3,19},{11,27},{4,20},{... | collective-permute-start | bytes 393224 | tf_op jit(solution)/shard_map/ppermute | solution.py:451
  80.8 9.0 %collective-permute-start.8 = (bf16[128,1024]{1,0:T(8,128)(2,1)S(1)}, bf16[128,1024]{1,0:T(8,128)(2,1)S(1)}, u32[]{:S(2)}, u32[]{:S(2)}) collective-permute-start(bf16[128,1024]{1,0:T(8,128)(2,1)S(1)} %get-tuple-element.65.own_ref), channel_id=1, source_target_pairs={{0,8},{8,0},{16,24},{24,16},{1,9},{9,1},{17,25},{25,17},{2,10},{10... | collective-permute-start | bytes 786440 | tf_op jit(solution)/shard_map/ppermute | solution.py:448
  84.8 8.0 %collective-permute-start.14 = (bf16[128,1024]{1,0:T(8,128)(2,1)S(1)}, bf16[128,1024]{1,0:T(8,128)(2,1)S(1)}, u32[]{:S(2)}, u32[]{:S(2)}) collective-permute-start(bf16[128,1024]{1,0:T(8,128)(2,1)S(1)} %get-tuple-element.72.own_ref), channel_id=1, source_target_pairs={{0,8},{8,0},{16,24},{24,16},{1,9},{9,1},{17,25},{25,17},{2,10},{10... | collective-permute-start | bytes 786440 | tf_op jit(solution)/shard_map/ppermute | solution.py:448
  96.7 202.7 %all-gather.14.cloned.1.call-start = ((), (), s32[]{:S(2)}) async-start(), calls=%async_computation.3 | async-start | bytes 4718592 | tf_op jit(solution)/shard_map/all_gather | solution.py:457
  105.6 7.5 %collective-permute-start.17 = (bf16[128,1024]{1,0:T(8,128)(2,1)S(1)}, bf16[128,1024]{1,0:T(8,128)(2,1)S(1)}, u32[]{:S(2)}, u32[]{:S(2)}) collective-permute-start(bf16[128,1024]{1,0:T(8,128)(2,1)S(1)} %feed_backward.4.refs_3_), channel_id=1, source_target_pairs={{0,8},{8,0},{16,24},{24,16},{1,9},{9,1},{17,25},{25,17},{2,10},{10... | collective-permute-start | bytes 786440 | tf_op jit(solution)/shard_map/ppermute | solution.py:448
  110.2 10.6 %collective-permute-start.23 = (bf16[128,1024]{1,0:T(8,128)(2,1)S(1)}, bf16[128,1024]{1,0:T(8,128)(2,1)S(1)}, u32[]{:S(2)}, u32[]{:S(2)}) collective-permute-start(bf16[128,1024]{1,0:T(8,128)(2,1)S(1)} %feed_backward.6.refs_3_), channel_id=1, source_target_pairs={{0,8},{8,0},{16,24},{24,16},{1,9},{9,1},{17,25},{25,17},{2,10},{10... | collective-permute-start | bytes 786440 | tf_op jit(solution)/shard_map/ppermute | solution.py:448
  119.8 7.8 %collective-permute-start.18 = (bf16[128,1024]{1,0:T(8,128)(2,1)S(1)}, bf16[128,1024]{1,0:T(8,128)(2,1)S(1)}, u32[]{:S(2)}, u32[]{:S(2)}) collective-permute-start(bf16[128,1024]{1,0:T(8,128)(2,1)S(1)} %get-tuple-element.76.own_ref), channel_id=1, source_target_pairs={{0,8},{8,0},{16,24},{24,16},{1,9},{9,1},{17,25},{25,17},{2,10},{10... | collective-permute-start | bytes 786440 | tf_op jit(solution)/shard_map/ppermute | solution.py:448
  125.9 6.4 %collective-permute-start.24 = (bf16[128,1024]{1,0:T(8,128)(2,1)S(1)}, bf16[128,1024]{1,0:T(8,128)(2,1)S(1)}, u32[]{:S(2)}, u32[]{:S(2)}) collective-permute-start(bf16[128,1024]{1,0:T(8,128)(2,1)S(1)} %get-tuple-element.83.own_ref), channel_id=1, source_target_pairs={{0,8},{8,0},{16,24},{24,16},{1,9},{9,1},{17,25},{25,17},{2,10},{10... | collective-permute-start | bytes 786440 | tf_op jit(solution)/shard_map/ppermute | solution.py:448
  128.6 10.5 %collective-permute-start.19 = (bf16[128,1024]{1,0:T(8,128)(2,1)}, bf16[128,1024]{1,0:T(8,128)(2,1)}, u32[]{:S(2)}, u32[]{:S(2)}) collective-permute-start(bf16[128,1024]{1,0:T(8,128)(2,1)} %get-tuple-element.77), channel_id=1, source_target_pairs={{16,0},{24,8},{17,1},{25,9},{18,2},{26,10},{19,3},{27,11},{20,4},{... | collective-permute-start | bytes 786440 | tf_op jit(solution)/shard_map/ppermute | solution.py:454
  134.0 8.8 %collective-permute-start.25 = (bf16[128,1024]{1,0:T(8,128)(2,1)}, bf16[128,1024]{1,0:T(8,128)(2,1)}, u32[]{:S(2)}, u32[]{:S(2)}) collective-permute-start(bf16[128,1024]{1,0:T(8,128)(2,1)} %get-tuple-element.84), channel_id=1, source_target_pairs={{16,0},{24,8},{17,1},{25,9},{18,2},{26,10},{19,3},{27,11},{20,4},{... | collective-permute-start | bytes 786440 | tf_op jit(solution)/shard_map/ppermute | solution.py:454
  146.7 205.8 %all-gather.16.cloned.1.call-start = ((), (), s32[]{:S(2)}) async-start(), calls=%async_computation.4 | async-start | bytes 2359296 | tf_op jit(solution)/shard_map/all_gather | solution.py:457
  146.7 7.1 %collective-permute-start.21 = (bf16[512,128]{1,0:T(8,128)(2,1)}, bf16[512,128]{1,0:T(8,128)(2,1)S(1)}, u32[]{:S(2)}, u32[]{:S(2)}) collective-permute-start(bf16[512,128]{1,0:T(8,128)(2,1)} %copy-done.66), channel_id=1, source_target_pairs={{16,0},{24,8},{17,1},{25,9},{18,2},{26,10},{19,3},{27,11},{20,4},{... | collective-permute-start | bytes 393224 | tf_op jit(solution)/shard_map/ppermute | solution.py:454
  148.0 7.2 %collective-permute-start.27 = (bf16[512,128]{1,0:T(8,128)(2,1)}, bf16[512,128]{1,0:T(8,128)(2,1)S(1)}, u32[]{:S(2)}, u32[]{:S(2)}) collective-permute-start(bf16[512,128]{1,0:T(8,128)(2,1)} %copy-done.67), channel_id=1, source_target_pairs={{16,0},{24,8},{17,1},{25,9},{18,2},{26,10},{19,3},{27,11},{20,4},{... | collective-permute-start | bytes 393224 | tf_op jit(solution)/shard_map/ppermute | solution.py:454
  156.6 195.9 %all-gather.12.cloned.1.call-start = ((), (), s32[]{:S(2)}) async-start(), calls=%async_computation.2 | async-start | bytes 4718592 | tf_op jit(solution)/shard_map/all_gather | solution.py:457
  167.0 8.6 %collective-permute-start.20 = (bf16[128,1024]{1,0:T(8,128)(2,1)S(1)}, bf16[128,1024]{1,0:T(8,128)(2,1)S(1)}, u32[]{:S(2)}, u32[]{:S(2)}) collective-permute-start(bf16[128,1024]{1,0:T(8,128)(2,1)S(1)} %feed_backward.5.refs_3_), channel_id=1, source_target_pairs={{0,8},{8,0},{16,24},{24,16},{1,9},{9,1},{17,25},{25,17},{2,10},{10... | collective-permute-start | bytes 786440 | tf_op jit(solution)/shard_map/ppermute | solution.py:448
  174.3 7.4 %collective-permute-start.26 = (bf16[128,1024]{1,0:T(8,128)(2,1)S(1)}, bf16[128,1024]{1,0:T(8,128)(2,1)S(1)}, u32[]{:S(2)}, u32[]{:S(2)}) collective-permute-start(bf16[128,1024]{1,0:T(8,128)(2,1)S(1)} %feed_backward.7.refs_3_), channel_id=1, source_target_pairs={{0,8},{8,0},{16,24},{24,16},{1,9},{9,1},{17,25},{25,17},{2,10},{10... | collective-permute-start | bytes 786440 | tf_op jit(solution)/shard_map/ppermute | solution.py:448
  214.3 48.8 %collective-permute-start.9 = (bf16[128,1024]{1,0:T(8,128)(2,1)S(1)}, bf16[128,1024]{1,0:T(8,128)(2,1)}, u32[]{:S(2)}, u32[]{:S(2)}) collective-permute-start(bf16[128,1024]{1,0:T(8,128)(2,1)S(1)} %copy-done.44), channel_id=1, source_target_pairs={{0,8},{8,0},{16,24},{24,16},{1,9},{9,1},{17,25},{25,17},{2,10},{10... | collective-permute-start | bytes 786440 | tf_op jit(solution)/shard_map/ppermute | solution.py:448
  223.5 40.7 %collective-permute-start.15 = (bf16[128,1024]{1,0:T(8,128)(2,1)S(1)}, bf16[128,1024]{1,0:T(8,128)(2,1)S(1)}, u32[]{:S(2)}, u32[]{:S(2)}) collective-permute-start(bf16[128,1024]{1,0:T(8,128)(2,1)S(1)} %copy-done.46), channel_id=1, source_target_pairs={{0,8},{8,0},{16,24},{24,16},{1,9},{9,1},{17,25},{25,17},{2,10},{10... | collective-permute-start | bytes 786440 | tf_op jit(solution)/shard_map/ppermute | solution.py:448
  264.3 7.1 %collective-permute-start.16 = (bf16[256,256]{1,0:T(8,128)(2,1)S(1)}, bf16[256,256]{1,0:T(8,128)(2,1)S(1)}, u32[]{:S(2)}, u32[]{:S(2)}) collective-permute-start(bf16[256,256]{1,0:T(8,128)(2,1)S(1)} %fusion.6), channel_id=1, source_target_pairs={{16,0},{24,8},{17,1},{25,9},{18,2},{26,10},{19,3},{27,11},{20,4},{... | collective-permute-start | bytes 393224 | tf_op jit(solution)/shard_map/ppermute | solution.py:454
  265.7 9.6 %collective-permute-start.22 = (bf16[128,1024]{1,0:T(8,128)(2,1)S(1)}, bf16[128,1024]{1,0:T(8,128)(2,1)S(1)}, u32[]{:S(2)}, u32[]{:S(2)}) collective-permute-start(bf16[128,1024]{1,0:T(8,128)(2,1)S(1)} %copy-done.50), channel_id=1, source_target_pairs={{0,8},{8,0},{16,24},{24,16},{1,9},{9,1},{17,25},{25,17},{2,10},{10... | collective-permute-start | bytes 786440 | tf_op jit(solution)/shard_map/ppermute | solution.py:448
  268.0 11.4 %collective-permute-start.28 = (bf16[128,1024]{1,0:T(8,128)(2,1)S(1)}, bf16[128,1024]{1,0:T(8,128)(2,1)S(1)}, u32[]{:S(2)}, u32[]{:S(2)}) collective-permute-start(bf16[128,1024]{1,0:T(8,128)(2,1)S(1)} %copy-done.54), channel_id=1, source_target_pairs={{0,8},{8,0},{16,24},{24,16},{1,9},{9,1},{17,25},{25,17},{2,10},{10... | collective-permute-start | bytes 786440 | tf_op jit(solution)/shard_map/ppermute | solution.py:448
  279.9 18.7 %collective-permute-start.29 = (bf16[256,256]{1,0:T(8,128)(2,1)S(1)}, bf16[256,256]{1,0:T(8,128)(2,1)S(1)}, u32[]{:S(2)}, u32[]{:S(2)}) collective-permute-start(bf16[256,256]{1,0:T(8,128)(2,1)S(1)} %dynamic-slice_convert_fusion), channel_id=1, source_target_pairs={{0,16},{8,24},{1,17},{9,25},{2,18},{10,26},{3,19},{11,27},{4,20},{... | collective-permute-start | bytes 393224 | tf_op jit(solution)/shard_map/ppermute | solution.py:451
  (87 other events, 1599.6 us)
Sparse Core Ops, SparseCore 0:
  22.3 47.9 all-gather.7
  72.5 45.9 all-gather.9
  120.1 46.1 all-gather.17
  168.4 46.1 all-gather.13
  216.0 28.2 all-gather.15
  245.7 46.8 all-gather.11

commit v2 on v1

v2 whole, which is shorter than its diff:
```python
import functools

import jax
import jax.numpy as jnp
from jax import lax
from jax.experimental import pallas as pl
from jax.experimental.pallas import tpu as pltpu
from jax.sharding import PartitionSpec as P

HEAD_DIM = 64
EPS = 1e-05
NEG = -1e30
GROUP = 8
BF = jnp.bfloat16
F32 = jnp.float32
MIB = 1024 * 1024


def dot_nn(left, right):
    return lax.dot_general(left, right, (((1,), (0,)), ((), ())), preferred_element_type=F32)


def dot_nt(left, right):
    return lax.dot_general(left, right, (((1,), (1,)), ((), ())), preferred_element_type=F32)


def dot_tn(left, right):
    return lax.dot_general(left, right, (((0,), (0,)), ((), ())), preferred_element_type=F32)


def shape_of(shape, dtype):
    return jax.ShapeDtypeStruct(shape, dtype)


def normalize(stream, axis):
    rscale = lax.rsqrt(jnp.mean(stream * stream, axis=axis, keepdims=True) + EPS)
    return stream * rscale, rscale


def norm_back(stream, grad_out, dact, gain):
    normed, rscale = normalize(stream, -1)
    scaled = dact * normed
    dnorm = dact * gain
    mean = jnp.mean(scaled * gain, axis=-1, keepdims=True)
    grad = grad_out + rscale * (dnorm - normed * mean)
    return grad, jnp.sum(scaled, axis=0, keepdims=True)


def turned(rows):
    return rows.astype(F32).T.astype(BF)


def allowed_keys(ends, count):
    key = lax.broadcasted_iota(jnp.int32, (count, count), 0)
    query = lax.broadcasted_iota(jnp.int32, (count, count), 1)
    segment_key = sum((key >= end).astype(jnp.int32) for end in ends)
    segment_query = sum((query >= end).astype(jnp.int32) for end in ends)
    return (key <= query) & (segment_key == segment_query)


def heads_of(array, first=0):
    return [array[at : at + HEAD_DIM] for at in range(first, array.shape[0], HEAD_DIM)]


def softmax_keys(scores, allowed):
    scores = jnp.where(allowed, scores * HEAD_DIM**-0.5, NEG)
    exponent = jnp.exp(scores - jnp.max(scores, axis=0, keepdims=True))
    return exponent * (1.0 / jnp.sum(exponent, axis=0, keepdims=True))


def attend(query, keys, values, allowed):
    query, keys, values = heads_of(query), heads_of(keys), heads_of(values)
    scores = [dot_tn(k, q) for q, k in zip(query, keys)]
    probs = [softmax_keys(s, allowed).astype(BF) for s in scores]
    return jnp.concatenate([dot_nn(v, p) for v, p in zip(values, probs)], axis=0)


def attend_back(query, keys, values, dattn, allowed, forward):
    query, keys, values, dattn = [heads_of(a) for a in (query, keys, values, dattn)]
    scores = [dot_tn(k, q) for q, k in zip(query, keys)]
    dprobs = [dot_tn(v, d) for v, d in zip(values, dattn)]
    low_probs, dscores = [], []
    for score, dprob in zip(scores, dprobs):
        probs = softmax_keys(score, allowed)
        low_probs.append(probs.astype(BF))
        dscores.append((probs * (dprob - jnp.sum(dprob * probs, axis=0, keepdims=True))).astype(BF))
    attn = None
    if forward:
        attn = jnp.concatenate([dot_nn(v, p) for v, p in zip(values, low_probs)], axis=0)
    dquery = jnp.concatenate([dot_nn(k, d) for k, d in zip(keys, dscores)], axis=0) * HEAD_DIM**-0.5
    dkeys = jnp.concatenate([dot_nt(q, d) for q, d in zip(query, dscores)], axis=0) * HEAD_DIM**-0.5
    dmixed = jnp.concatenate([dot_nt(d, p) for d, p in zip(dattn, low_probs)], axis=0)
    return dquery, dkeys, dmixed, attn


def swish(gate, up):
    sigmoid = 1.0 / (1.0 + jnp.exp(-gate))
    return sigmoid, gate * sigmoid


def feed_back(gate, up, dhid):
    sigmoid, silu = swish(gate, up)
    hid = (silu * up).astype(BF)
    dgate = dhid * up * (sigmoid * (1.0 + gate * (1.0 - sigmoid)))
    dup = dhid * silu
    return hid, dgate.astype(BF), dup.astype(BF)


def ends_at(ends_ref, slot):
    return [ends_ref[slot, i] for i in range(ends_ref.shape[1])]


def rounded_sum(left, right):
    return left.astype(F32) + right.astype(F32)


def turn_kernel(a_ref, b_ref, a_out, b_out):
    size = 256
    row = lax.broadcasted_iota(jnp.int32, (size, size), 0)
    col = lax.broadcasted_iota(jnp.int32, (size, size), 1)
    identity = jnp.where(row == col, 1.0, 0.0).astype(BF)
    for source, target in ((a_ref, a_out), (b_ref, b_out)):
        for at in range(0, source.shape[1], size):
            target[at : at + size, :] = dot_nt(identity, source[:, at : at + size]).astype(BF)


def attn_first_kernel(slot, ends_ref, x_ref, gain_ref, inward_ref, outward_ref, part_ref, values_ref, square_ref):
    count = x_ref.shape[0]
    width = outward_ref.shape[0]
    normed, unused = normalize(x_ref[...].astype(F32), -1)
    act = (normed * gain_ref[...]).astype(BF)
    proj = dot_nn(act, inward_ref[...]).T.astype(BF)
    values = proj[2 * width :]
    values_ref[...] = values
    wide = values.astype(F32)
    square_ref[...] = jnp.sum(wide * wide, axis=0, keepdims=True)
    allowed = allowed_keys(ends_at(ends_ref, slot), count)
    attn = attend(proj[:width], proj[width : 2 * width], values, allowed)
    part_ref[...] = dot_nn(attn.T.astype(BF), outward_ref[...]).astype(BF)


def feed_first_kernel(
    own_ref,
    mate_ref,
    part_own_ref,
    part_mate_ref,
    got_own_ref,
    got_mate_ref,
    gain_ref,
    inward_ref,
    outward_ref,
    mid_own_ref,
    mid_mate_ref,
    turned_ref,
    send_own_ref,
    send_mate_ref,
):
    count = own_ref.shape[0]
    own = (own_ref[...].astype(F32) + rounded_sum(part_own_ref[...], got_own_ref[...])).astype(BF)
    mate = (mate_ref[...].astype(F32) + rounded_sum(part_mate_ref[...], got_mate_ref[...])).astype(BF)
    mid_own_ref[...] = own
    mid_mate_ref[...] = mate
    turned_ref[0] = turned(own)
    turned_ref[1] = turned(mate)
    stream = jnp.concatenate([own, mate], axis=0).astype(F32)
    normed, unused = normalize(stream, -1)
    act = (normed * gain_ref[...]).astype(BF)
    hidden = outward_ref.shape[0]
    gate = dot_nn(act, inward_ref[:, :hidden])
    up = dot_nn(act, inward_ref[:, hidden:])
    unused, silu = swish(gate, up)
    part = dot_nn((silu * up).astype(BF), outward_ref[...])
    send_own_ref[...] = (stream[:count] + part[:count]).astype(BF)
    send_mate_ref[...] = part[count:].astype(BF)


def attn_second_kernel(
    ends_ref,
    a_ref,
    b_ref,
    gain_ref,
    inward_ref,
    inward_mate_ref,
    outward_ref,
    outward_mate_ref,
    mix_ref,
    mix_mate_ref,
    first_ref,
    first_mate_ref,
    x_ref,
    turned_ref,
    mid_ref,
    square_ref,
):
    count = a_ref.shape[0]
    width = outward_ref.shape[0]
    x = rounded_sum(a_ref[...], b_ref[...]).astype(BF)
    x_ref[...] = x
    turned_ref[...] = turned(x)
    stream = x.astype(F32)
    normed, unused = normalize(stream, -1)
    act = (normed * gain_ref[...]).astype(BF)
    allowed = allowed_keys(ends_at(ends_ref, 0), count)
    square = 0.0
    for w_in, w_out, m_ref, f_ref in (
        (inward_ref, outward_ref, mix_ref, first_ref),
        (inward_mate_ref, outward_mate_ref, mix_mate_ref, first_mate_ref),
    ):
        proj = dot_nn(act, w_in[...]).T.astype(BF)
        mix = m_ref[...]
        mixed = (1.0 - mix) * proj[2 * width :].astype(F32) + mix * f_ref[...].astype(F32)
        mixed = mixed.astype(BF)
        wide = mixed.astype(F32)
        square = square + jnp.sum(wide * wide, axis=0, keepdims=True)
        attn = attend(proj[:width], proj[width : 2 * width], mixed, allowed)
        stream = stream + dot_nn(attn.T.astype(BF), w_out[...])
    mid_ref[...] = stream.astype(BF)
    square_ref[...] = square


def feed_second_kernel(
    own_ref,
    mate_ref,
    grad_own_ref,
    grad_mate_ref,
    gain_ref,
    inward_ref,
    outward_ref,
    part_own_ref,
    part_mate_ref,
    turned_ref,
    out_own_ref,
    out_mate_ref,
):
    count = own_ref.shape[0]
    turned_ref[0] = turned(own_ref[...])
    turned_ref[1] = turned(mate_ref[...])
    stream = jnp.concatenate([own_ref[...], mate_ref[...]], axis=0).astype(F32)
    grad = jnp.concatenate([grad_own_ref[...], grad_mate_ref[...]], axis=0)
    normed, unused = normalize(stream, -1)
    act = (normed * gain_ref[...]).astype(BF)
    hidden = outward_ref.shape[0]
    gate = dot_nn(act, inward_ref[:, :hidden])
    up = dot_nn(act, inward_ref[:, hidden:])
    dhid = dot_nt(grad, outward_ref[...])
    hid, dgate, dup = feed_back(gate, up, dhid)
    dact = dot_nt(dgate, inward_ref[:, :hidden]) + dot_nt(dup, inward_ref[:, hidden:])
    part_own_ref[...] = dact[:count].astype(BF)
    part_mate_ref[...] = dact[count:].astype(BF)
    part = dot_nn(hid, outward_ref[...])
    out_own_ref[...] = stream[:count] + part[:count]
    out_mate_ref[...] = part[count:].astype(BF)


def feed_first_back_kernel(
    own_ref,
    mate_ref,
    grad_own_ref,
    grad_mate_ref,
    gain_ref,
    inward_ref,
    outward_ref,
    part_own_ref,
    part_mate_ref,
    turned_ref,
):
    count = own_ref.shape[0]
    turned_ref[0] = turned(grad_own_ref[...])
    turned_ref[1] = turned(grad_mate_ref[...])
    stream = jnp.concatenate([own_ref[...], mate_ref[...]], axis=0).astype(F32)
    grad = jnp.concatenate([grad_own_ref[...], grad_mate_ref[...]], axis=0)
    normed, unused = normalize(stream, -1)
    act = (normed * gain_ref[...]).astype(BF)
    hidden = outward_ref.shape[0]
    gate = dot_nn(act, inward_ref[:, :hidden])
    up = dot_nn(act, inward_ref[:, hidden:])
    dhid = dot_nt(grad, outward_ref[...])
    unused, dgate, dup = feed_back(gate, up, dhid)
    dact = dot_nt(dgate, inward_ref[:, :hidden]) + dot_nt(dup, inward_ref[:, hidden:])
    part_own_ref[...] = dact[:count].astype(BF)
    part_mate_ref[...] = dact[count:].astype(BF)


def attn_back_kernel(mixing, *refs):
    (
        ends_ref,
        mid_ref,
        grad_next_ref,
        part_ref,
        got_ref,
        gain_feed_ref,
        x_ref,
        gain_ref,
        inward_ref,
        inward_mate_ref,
        outward_ref,
        outward_mate_ref,
        mix_ref,
        mix_mate_ref,
        first_ref,
        first_mate_ref,
    ) = refs[:16]
    turned_ref, grad_ref, dgain_feed_ref, dgain_ref = refs[16:20]
    dfirst_refs = refs[20:]
    count = x_ref.shape[0]
    width = outward_ref.shape[0]
    dact_next = rounded_sum(part_ref[...], got_ref[...])
    grad, dgain = norm_back(
        mid_ref[...].astype(F32), grad_next_ref[...].astype(F32), dact_next, gain_feed_ref[...]
    )
    dgain_feed_ref[...] = dgain
    low_grad = grad.astype(BF)
    grad = low_grad.astype(F32)
    turned_ref[...] = grad.T.astype(BF)
    stream = x_ref[...].astype(F32)
    normed, unused = normalize(stream, -1)
    act = (normed * gain_ref[...]).astype(BF)
    allowed = allowed_keys(ends_at(ends_ref, 0), count)
    dact = 0.0
    for i, (w_in, w_out, m_ref, f_ref) in enumerate(
        (
            (inward_ref, outward_ref, mix_ref, first_ref),
            (inward_mate_ref, outward_mate_ref, mix_mate_ref, first_mate_ref),
        )
    ):
        dattn = dot_nt(low_grad, w_out[...]).T.astype(BF)
        proj = dot_nn(act, w_in[...]).T.astype(BF)
        values = proj[2 * width :]
        if mixing:
            mix = m_ref[...]
            values = ((1.0 - mix) * values.astype(F32) + mix * f_ref[...].astype(F32)).astype(BF)
        dquery, dkeys, dmixed, unused = attend_back(
            proj[:width], proj[width : 2 * width], values, dattn, allowed, False
        )
        if mixing:
            dfirst_refs[i][...] = (mix * dmixed).astype(BF)
            dvalues = (1.0 - mix) * dmixed
        else:
            dvalues = dmixed + f_ref[...].astype(F32)
        dproj = jnp.concatenate([dquery, dkeys, dvalues], axis=0).T.astype(BF)
        dact = dact + dot_nt(dproj, w_in[...])
    grad, dgain = norm_back(stream, grad, dact, gain_ref[...])
    grad_ref[...] = grad.astype(grad_ref.dtype)
    dgain_ref[...] = dgain


def call(kernel, outs, *args, smem=0, flops=0, name=None):
    moved = sum(a.size * a.dtype.itemsize for a in args) + sum(o.size * o.dtype.itemsize for o in outs)
    return pl.pallas_call(
        kernel,
        out_shape=outs,
        in_specs=[pl.BlockSpec(memory_space=pltpu.SMEM)] * smem
        + [pl.BlockSpec(memory_space=pltpu.VMEM)] * (len(args) - smem),
        out_specs=[pl.BlockSpec(memory_space=pltpu.VMEM)] * len(outs),
        compiler_params=pltpu.CompilerParams(vmem_limit_bytes=40 * MIB),
        cost_estimate=pl.CostEstimate(flops=int(flops), bytes_accessed=int(moved), transcendentals=0),
        name=name,
    )(*args)


def block_ref(refs, block):
    operand, index = block
    return refs[operand] if index is None else refs[operand].at[index]


def fetch(pick, refs, choices, target, sems):
    for which, blocks in enumerate(choices):

        @pl.when(pick == which)
        def _():
            for at, block in enumerate(blocks):
                source = block_ref(refs, block)
                count = source.shape[1]
                pltpu.make_async_copy(source, target.at[:, at * count : (at + 1) * count], sems.at[at]).start()


def arrived(refs, blocks, target, sems, at):
    source = block_ref(refs, blocks[0])
    count = source.shape[1]
    place = pl.ds(pl.multiple_of(at * count, count), count)
    pltpu.make_async_copy(source, target.at[:, place], sems.at[at]).wait()


def write_out(stage, sems, target, step, value):
    size = stage.shape[2]
    slot = lax.rem(step, 2)
    place = pl.ds(pl.multiple_of(step * size, size), size)
    copy = pltpu.make_async_copy(stage.at[slot], target.at[:, place], sems.at[slot])

    @pl.when(step >= 2)
    def _():
        copy.wait()

    stage[slot] = value.astype(stage.dtype)
    copy.start()


def written(stage, sems, target, steps):
    size = stage.shape[2]
    for step in range(max(steps - 2, 0), steps):
        slot = step % 2
        pltpu.make_async_copy(
            stage.at[slot], target.at[:, step * size : (step + 1) * size], sems.at[slot]
        ).wait()


def products(left, right, stage, sems, target):
    size = stage.shape[2]
    steps = right.shape[0] // size

    def one(step, unused):
        rows = pl.ds(pl.multiple_of(step * size, size), size)
        write_out(stage, sems, target, step, dot_nt(left[...], right[rows, :]))
        return 0

    lax.fori_loop(0, steps, one, 0)
    return steps


def feed_weights_kernel(layout, *refs):
    (streams, grads), operands = layout
    pick_ref = refs[0]
    blocks_refs = refs[1 : 1 + operands]
    gain_ref, inward_ref, outward_ref = refs[1 + operands : 4 + operands]
    dinward_ref, doutward_ref = refs[4 + operands : 6 + operands]
    act_all, grad_all, hid_all, dboth_all, stage_in, stage_out, sems, out_sems = refs[6 + operands :]
    hidden = outward_ref.shape[0]
    pick = pick_ref[0]
    fetch(pick, blocks_refs, streams, act_all, sems.at[0])
    fetch(pick, blocks_refs, grads, grad_all, sems.at[1])
    blocks = len(streams[0])
    wider = 2 * (act_all.shape[1] // blocks)

    def rows(step, unused):
        for at in (2 * step, 2 * step + 1):
            arrived(blocks_refs, streams[0], act_all, sems.at[0], at)
            arrived(blocks_refs, grads[0], grad_all, sems.at[1], at)
        here = pl.ds(pl.multiple_of(step * wider, wider), wider)
        normed, unused = normalize(act_all[:, here].astype(F32), 0)
        act = (normed * gain_ref[...]).astype(BF)
        act_all[:, here] = act
        both = dot_nn(inward_ref[...], act)
        dhid = dot_nn(outward_ref[...], grad_all[:, here])
        hid, dgate, dup = feed_back(both[:hidden], both[hidden:], dhid)
        hid_all[:, here] = hid
        dboth_all[:hidden, here] = dgate
        dboth_all[hidden:, here] = dup
        return 0

    lax.fori_loop(0, blocks // 2, rows, 0)
    wide = products(act_all, dboth_all, stage_in, out_sems.at[0], dinward_ref)
    across = products(hid_all, grad_all, stage_out, out_sems.at[1], doutward_ref)
    written(stage_in, out_sems.at[0], dinward_ref, wide)
    written(stage_out, out_sems.at[1], doutward_ref, across)


def attn_weights_kernel(layout, *refs):
    (streams, grads, firsts), operands = layout
    pick_ref, ends_ref = refs[:2]
    blocks_refs = refs[2 : 2 + operands]
    gain_ref, mix_ref, add_ref, inward_ref, outward_ref = refs[2 + operands : 7 + operands]
    dinward_ref, doutward_ref = refs[7 + operands : 9 + operands]
    act_all, grad_all, attn_all, dproj_all, first_all, stage_in, stage_out, sems, out_sems = refs[9 + operands :]
    width = outward_ref.shape[0]
    pick = pick_ref[0]
    fetch(pick, blocks_refs, streams, act_all, sems.at[0])
    fetch(pick, blocks_refs, grads, grad_all, sems.at[1])
    fetch(pick, blocks_refs, firsts, first_all, sems.at[2])
    blocks = len(streams[0])
    count = act_all.shape[1] // blocks
    wider = 2 * count

    def rows(step, unused):
        for at in (2 * step, 2 * step + 1):
            arrived(blocks_refs, streams[0], act_all, sems.at[0], at)
            arrived(blocks_refs, grads[0], grad_all, sems.at[1], at)
            arrived(blocks_refs, firsts[0], first_all, sems.at[2], at)
        here = pl.ds(pl.multiple_of(step * wider, wider), wider)
        normed, unused = normalize(act_all[:, here].astype(F32), 0)
        act = (normed * gain_ref[...]).astype(BF)
        act_all[:, here] = act
        proj = dot_nn(inward_ref[...], act).astype(BF)
        dattn = dot_nn(outward_ref[...], grad_all[:, here]).astype(BF)
        first = first_all[:, here].astype(F32)
        mix = mix_ref[...]
        values = ((1.0 - mix) * proj[2 * width :].astype(F32) + mix * first).astype(BF)
        for i in range(2):
            cols = slice(i * count, (i + 1) * count)
            place = pl.ds(pl.multiple_of(step * wider + i * count, count), count)
            allowed = allowed_keys(ends_at(ends_ref, step * 2 + i), count)
            dquery, dkeys, dmixed, attn = attend_back(
                proj[:width, cols],
                proj[width : 2 * width, cols],
                values[:, cols],
                dattn[:, cols],
                allowed,
                True,
            )
            dvalues = (1.0 - mix) * dmixed + add_ref[...] * first[:, cols]
            attn_all[:, place] = attn.astype(BF)
            dproj_all[:, place] = jnp.concatenate([dquery, dkeys, dvalues], axis=0).astype(BF)
        return 0

    lax.fori_loop(0, blocks // 2, rows, 0)
    wide = products(act_all, dproj_all, stage_in, out_sems.at[0], dinward_ref)
    across = products(attn_all, grad_all, stage_out, out_sems.at[1], doutward_ref)
    written(stage_in, out_sems.at[0], dinward_ref, wide)
    written(stage_out, out_sems.at[1], doutward_ref, across)


def weight_call(kernel, smem, sets, small, weights, name, block=256):
    arrays, layout = [], []
    for choices in sets:
        placed = []
        for blocks in choices:
            row = []
            for array, index in blocks:
                at = next((i for i, a in enumerate(arrays) if a is array), None)
                if at is None:
                    at = len(arrays)
                    arrays.append(array)
                row.append((at, index))
            placed.append(tuple(row))
        layout.append(tuple(placed))
    inward, outward = weights
    model = inward.shape[1]
    blocks = len(layout[0][0])
    total = blocks * arrays[0].shape[-1]
    extra = [pltpu.VMEM((outward.shape[0], total), BF)] if len(sets) == 3 else []
    flops = 4 * total * (inward.size + outward.size)
    any_spec, vmem_spec = pl.BlockSpec(memory_space=pl.ANY), pl.BlockSpec(memory_space=pltpu.VMEM)
    return pl.pallas_call(
        functools.partial(kernel, (tuple(layout), len(arrays))),
        in_specs=[pl.BlockSpec(memory_space=pltpu.SMEM)] * len(smem)
        + [any_spec] * len(arrays)
        + [vmem_spec] * (len(small) + 2),
        out_specs=[any_spec] * 2,
        out_shape=[
            shape_of((model, inward.shape[0]), BF),
            shape_of((outward.shape[0], model), BF),
        ],
        scratch_shapes=[
            pltpu.VMEM((model, total), BF),
            pltpu.VMEM((model, total), BF),
            pltpu.VMEM((outward.shape[0], total), BF),
            pltpu.VMEM((inward.shape[0], total), BF),
        ]
        + extra
        + [
            pltpu.VMEM((2, model, block), BF),
            pltpu.VMEM((2, outward.shape[0], block), BF),
            pltpu.SemaphoreType.DMA((len(sets), blocks)),
            pltpu.SemaphoreType.DMA((2, 2)),
        ],
        compiler_params=pltpu.CompilerParams(vmem_limit_bytes=44 * MIB),
        cost_estimate=pl.CostEstimate(flops=flops, bytes_accessed=16 * MIB, transcendentals=0),
        name=name,
    )(*smem, *arrays, *small, *weights)


def body(tokens, cotangent, gains, attn_in, attn_out, ffn_in, ffn_out, mix_level, seq_lengths):
    section = lax.axis_index("section")
    core = lax.axis_index("dp") % 2
    lower = section < 2
    even = section % 2 == 0
    sections = lax.axis_size("section")
    dp = lax.axis_size("dp")
    group = min(dp, GROUP)
    planes = group // 2
    micro = seq_lengths.shape[0]
    count = tokens.shape[0] // micro
    piece = tokens.shape[1]
    inward, outward, feed_in, feed_out = attn_in[0], attn_out[0], ffn_in[0], ffn_out[0]
    model = inward.shape[0]
    width = outward.shape[0]

    def send(x, mask, sources=(0, 1, 2, 3)):
        return lax.ppermute(x, "section", [(i, i ^ mask) for i in sources])

    def plane(x, by):
        pairs = [
            (i, i // group * group + (i % group // 2 + by) % planes * 2 + i % 2) for i in range(dp)
        ]
        return lax.ppermute(x, "dp", pairs)

    def planes_of(x):
        return [plane(x, by) for by in range(1, planes)]

    def other_core(x):
        return lax.ppermute(x, "dp", [(i, i ^ 1) for i in range(dp)])

    low, high = (0, 1), (2, 3)

    near = jnp.where(lower, tokens, cotangent)
    far = jnp.where(lower, cotangent, tokens)
    got_near, got_far, got_across = send(near, 1), send(far, 2), send(far, 3)
    got_gains = send(gains, 1)
    ends = jnp.cumsum(seq_lengths, axis=1)
    ends = jnp.where(even, ends, ends[::-1])
    all_ends = jnp.concatenate([ends] + planes_of(ends), axis=0)
    feed_in_turned, inward_turned = call(
        turn_kernel,
        [shape_of(feed_in.shape[::-1], BF), shape_of(inward.shape[::-1], BF)],
        feed_in,
        inward,
        flops=2 * 256 * (feed_in.size + inward.size),
        name="turn_weights",
    )

    def by_half(mine, other):
        return [jnp.where(even, mine, other), jnp.where(even, other, mine)]

    ours, theirs = by_half(near, got_near), by_half(got_far, got_across)
    given = jnp.concatenate(
        [jnp.where(lower, a, b) for a, b in zip(ours + theirs, theirs + ours)], axis=1
    )
    top, bottom = given[:count], given[count:]
    given_own, given_mate = jnp.where(even, top, bottom), jnp.where(even, bottom, top)
    given_turned = jnp.stack([given_own.T, given_mate.T])

    gain_attn = jnp.where(even, gains, got_gains)
    gain_feed = jnp.where(even, got_gains, gains)
    mix_all = jnp.repeat(mix_level.astype(F32) / 8.0, HEAD_DIM)
    mix_low, mix_high = mix_all[:width, None], mix_all[width:, None]
    mix, mix_mate = jnp.where(even, mix_low, mix_high), jnp.where(even, mix_high, mix_low)

    def swapped_weights(w_in, w_out, sources):
        def parts(w):
            half = w.shape[0] // 2
            mine = send(lax.dynamic_slice_in_dim(w, core * half, half, 0), 1, sources)
            other = other_core(mine)
            return jnp.where(
                core == 0,
                jnp.concatenate([mine, other], axis=0),
                jnp.concatenate([other, mine], axis=0),
            )

        return parts(w_in), parts(w_out)

    inward_high, outward_high = swapped_weights(inward, outward, high)

    attn_flops = 2 * count * (inward.size + outward.size)
    feed_flops = 4 * count * (feed_in.size + feed_out.size)
    slot = shape_of((count, model), BF)
    slot_wide = shape_of((count, model), F32)
    half_turned = shape_of((width, count), BF)
    slot_turned = shape_of((model, count), BF)
    pair_turned = shape_of((2, model, count), BF)
    row = shape_of((1, model), F32)
    square_row = shape_of((1, count), F32)

    def attn_first(which, x):
        return call(
            functools.partial(attn_first_kernel, which),
            [slot, half_turned, square_row],
            ends,
            x,
            gain_attn,
            inward,
            outward,
            smem=1,
            flops=attn_flops,
            name="attn_first",
        )

    part_mate, first_mate, square_mate = attn_first(1, given_mate)
    got_own = send(part_mate, 1, low)
    part_own, first_own, square_own = attn_first(0, given_own)
    got_mate = send(part_own, 1, low)
    mid0_own, mid0_mate, mid0_turned, send_own, send_mate = call(
        feed_first_kernel,
        [slot, slot, pair_turned, slot, slot],
        given_own,
        given_mate,
        part_own,
        part_mate,
        got_own,
        got_mate,
        gain_feed,
        feed_in,
        feed_out,
        flops=feed_flops,
        name="feed_first",
    )
    x_a, x_b = send(send_own, 2, low), send(send_mate, 3, low)
    first_a, first_b, first_c = (
        send(first_own, 2, low),
        send(first_mate, 3, low),
        send(first_mate, 2, low),
    )

    x1, x1_turned, mid1_own, square1 = call(
        attn_second_kernel,
        [slot, slot_turned, slot, square_row],
        ends,
        x_a,
        x_b,
        gain_attn,
        inward,
        inward_high,
        outward,
        outward_high,
        mix,
        mix_mate,
        first_a,
        first_b,
        smem=1,
        flops=2 * attn_flops,
        name="attn_second",
    )
    mid1_mate = send(mid1_own, 1, high)
    part_own, part_mate, mid1_turned, out_own, out_mate = call(
        feed_second_kernel,
        [slot, slot, pair_turned, slot_wide, slot],
        mid1_own,
        mid1_mate,
        given_own,
        given_mate,
        gain_feed,
        feed_in,
        feed_out,
        flops=3 * feed_flops,
        name="feed_second",
    )
    got_own = send(part_mate, 1, high)
    got_out = send(out_mate, 1, high)

    def attn_back(mixing, mid, grad_next, part, got, x, w_in_mate, w_out_mate, first, mate, dtype):
        return call(
            functools.partial(attn_back_kernel, mixing),
            [slot_turned, shape_of((count, model), dtype), row, row] + [half_turned] * (2 * mixing),
            ends,
            mid,
            grad_next,
            part,
            got,
            gain_feed,
            x,
            gain_attn,
            inward,
            w_in_mate,
            outward,
            w_out_mate,
            mix,
            mix_mate,
            first,
            mate,
            smem=1,
            flops=5 * attn_flops,
            name="attn_back",
        )

    grad1_turned, grad_x1, dgain_feed1, dgain_attn1, dfirst, dfirst_mate = attn_back(
        True,
        mid1_own,
        given_own,
        part_own,
        got_own,
        x1,
        inward_high,
        outward_high,
        first_a,
        first_b,
        BF,
    )
    grad_own, grad_mate = send(grad_x1, 2, high), send(grad_x1, 3, high)
    dfirst_a, dfirst_b, dfirst_c = (
        send(dfirst, 2, high),
        send(dfirst_mate, 2, high),
        send(dfirst_mate, 3, high),
    )

    late_in, late_out, unused = lax.optimization_barrier((inward, outward, send_own))
    inward_low, outward_low = swapped_weights(late_in, late_out, low)
    part_own, part_mate, grad0_turned = call(
        feed_first_back_kernel,
        [slot, slot, pair_turned],
        mid0_own,
        mid0_mate,
        grad_own,
        grad_mate,
        gain_feed,
        feed_in,
        feed_out,
        flops=2 * feed_flops,
        name="feed_first_back",
    )
    got_own = send(part_mate, 1, low)
    grad_mid0_turned, dinput, dgain_feed0, dgain_attn0 = attn_back(
        False,
        mid0_own,
        grad_own,
        part_own,
        got_own,
        given_own,
        inward_low,
        outward_low,
        dfirst_a,
        dfirst_b,
        F32,
    )

    def pairs_known(stacked):
        return [(a, i) for a in [stacked] + planes_of(stacked) for i in range(2)]

    def pairs_swapped(own, mate):
        got = planes_of(own)
        blocks = [(own, None), (mate, None)]
        for x in got:
            blocks += [(x, None), (send(x, 1), None)]
        return blocks

    set_given = pairs_known(given_turned)
    set_second = pairs_swapped(
        jnp.where(lower, mid0_turned[0], x1_turned),
        jnp.where(lower, mid0_turned[1], send(x1_turned, 1, high)),
    )
    set_first = pairs_known(
        jnp.stack([jnp.where(lower, dfirst_a, first_a), jnp.where(lower, dfirst_c, first_c)])
    )
    set_third = pairs_swapped(mid1_turned[0], mid1_turned[1])
    set_fourth = pairs_swapped(
        jnp.where(lower, grad0_turned[0], grad1_turned),
        jnp.where(lower, grad0_turned[1], send(grad1_turned, 1, high)),
    )
    set_fifth = pairs_swapped(grad_mid0_turned, send(grad_mid0_turned, 1, low))

    pick = jnp.where(lower, 0, 1).astype(jnp.int32)[None]
    d_feed_in, d_feed_out = weight_call(
        feed_weights_kernel,
        (pick,),
        ((set_second, set_third), (set_fourth, set_given)),
        (gain_feed.reshape(model, 1),),
        (feed_in_turned, feed_out),
        "feed_weights",
    )
    got_feed_in, got_feed_out = other_core(d_feed_in), other_core(d_feed_out)
    d_in, d_out = weight_call(
        attn_weights_kernel,
        (pick, all_ends),
        ((set_given, set_second), (set_fifth, set_fourth), (set_first, set_first)),
        (
            gain_attn.reshape(model, 1),
            jnp.where(lower, 0.0, mix),
            jnp.where(lower, jnp.ones_like(mix), 0.0),
        ),
        (inward_turned, outward),
        "attn_weights",
    )
    got_in, got_out_weights = other_core(d_in), other_core(d_out)

    def over_groups(x):
        if dp == group:
            return x
        across = [list(range(at, dp, group)) for at in range(group)]
        return lax.psum(x.astype(BF), "dp", axis_index_groups=across).astype(F32)

    d_in, d_out, d_feed_in, d_feed_out = [
        over_groups(rounded_sum(a, b))[None]
        for a, b in (
            (d_in, got_in),
            (d_out, got_out_weights),
            (d_feed_in, got_feed_in),
            (d_feed_out, got_feed_out),
        )
    ]

    dgain_attn = jnp.where(lower, dgain_attn0, dgain_attn1)
    dgain_feed = jnp.where(lower, dgain_feed0, dgain_feed1)
    dgain = jnp.where(even, dgain_attn, dgain_feed) + send(jnp.where(even, dgain_feed, dgain_attn), 1)
    square0 = square_own + square_mate
    squares = jnp.concatenate(
        [
            jnp.where(lower, jnp.sum(square0), 0.0)[None],
            jnp.where(lower, 0.0, jnp.sum(square1))[None],
            jnp.zeros((126,), F32),
        ]
    )[None]
    sums = jnp.concatenate([dgain, squares], axis=1)
    sums = sum(planes_of(sums), sums)
    sums = sums + other_core(sums)
    if dp > group:
        sums = lax.psum(sums, "dp") / group
    d_gain, squares = sums[:, :model], sums[0, model:]
    squares = squares + send(squares, 1) + send(squares, 2) + send(squares, 3)
    norms = squares[:2] / (micro * count * dp * 2 * width)

    def owners(rows, holders):
        def part(mask):
            return lax.dynamic_slice_in_dim(rows, (section ^ mask) * piece, piece, 1)

        held = lower if holders == low else ~lower
        beside, over, across = [send(part(mask), mask, holders) for mask in (1, 2, 3)]
        own, mate = jnp.where(held, part(0), over), jnp.where(held, beside, across)
        return jnp.where(
            even, jnp.concatenate([own, mate], axis=0), jnp.concatenate([mate, own], axis=0)
        )

    out = owners((out_own + got_out.astype(F32)).astype(BF), high)
    dinput = owners(dinput.astype(BF), low).astype(F32)
    return (out, dinput, d_gain, d_in, d_out, d_feed_in, d_feed_out, norms[0], norms[1])


def solution(mesh):
    in_specs = (
        P("dp", "section"),
        P("dp", "section"),
        P("section", None),
        P("section", None, None),
        P("section", None, None),
        P("section", None, None),
        P("section", None, None),
        P(),
        P("dp", None),
    )
    out_specs = (
        P("dp", "section"),
        P("dp", "section"),
        P("section", None),
        P("section", None, None),
        P("section", None, None),
        P("section", None, None),
        P("section", None, None),
        P(),
        P(),
    )
    return jax.shard_map(body, mesh=mesh, in_specs=in_specs, out_specs=out_specs, check_vma=False)
```

time: 449 us -> 471 us (1.049)
  Pallas kernels: 195 us -> 99.1 us
  starting transfers between devices: 50 us -> 139 us
  waiting for transfers between devices: 49.6 us -> 125 us
  blocking collectives: 65.2 us -> 0 us
  other arithmetic: 13.9 us -> 45.9 us
  between operations: 18.3 us -> 3.63 us
    pallas_call x22 -> x11, Pallas kernels: 195 us -> 99.1 us  [the longest x2 56.7 us: weight_call(): pl.pallas_call(functools.partial(kernel, (tuple(layout), len(arrays))), i...]
    ppermute x30 -> x82, starting transfers between devices: 49.4 us -> 139 us  [the longest x49 85.8 us: send(): return lax.ppermute(x, 'section', [(i, i ^ mask) for i in sources])]
    ppermute x30 -> x82, waiting for transfers between devices: 49.5 us -> 125 us  [the longest x49 103 us: send(): return lax.ppermute(x, 'section', [(i, i ^ mask) for i in sources])]
    psum x2 -> x0, blocking collectives: 52.7 us -> none  [the longest x1 38.3 us: body(): lax.psum(squares, ('section', 'dp')) / (micro * count * dp * 2 * width)]
    broadcast_in_dim x0 -> x5, other arithmetic: none -> 23.2 us  [the longest x4 22.6 us: body(): over_groups(rounded_sum(a, b))[None]]
    all_gather x1 -> x0, blocking collectives: 12.5 us -> none  [body(): lax.all_gather(ends, 'dp', axis=0, tiled=True, axis_index_groups=groups)]
    select_n x4 -> x15, other arithmetic: 1.53 us -> 13.6 us  [the longest x4 11.6 us: parts(): jnp.where(core == 0, jnp.concatenate([mine, other], axis=0), jnp.concaten...]
    unnamed x169 -> x150, local copies, waits for them, and re-layouts: 34.7 us -> 27.9 us
  transfers between devices with their start and end apart: 36 -> 82, of which waited for: 23 -> 23; matrix products, arithmetic and copies ran while one was open for 8% -> 12% of each run, Pallas kernels for 26% -> 21%
where the time goes in v2:
time: 471 us; the launch traced here: 461 us
  starting transfers between devices  139 us (30%)
  waiting for transfers between devices  125 us (27%)
  Pallas kernels  99.1 us (21%)
  local copies, waits for them, and re-layouts  48.6 us (10%)
  other arithmetic  45.9 us (10%)
    ppermute x49, waiting for transfers between devices, send(): return lax.ppermute(x, 'section', [(i, i ^ mask) for i in sources])  103 us
    ppermute x49, starting transfers between devices, send(): return lax.ppermute(x, 'section', [(i, i ^ mask) for i in sources])  85.8 us
    pallas_call x2, Pallas kernels, weight_call(): pl.pallas_call(functools.partial(kernel, (tuple(layout), len(arrays))), i...  56.7 us
    ppermute x24, starting transfers between devices, plane(): return lax.ppermute(x, 'dp', pairs)  52.3 us
    pallas_call x9, Pallas kernels, call(): pl.pallas_call(kernel, out_shape=outs, in_specs=[pl.BlockSpec(memory_spac...  42.5 us
    unnamed x150, local copies, waits for them, and re-layouts  27.9 us
    broadcast_in_dim x4, other arithmetic, body(): over_groups(rounded_sum(a, b))[None]  22.6 us
    ppermute x24, waiting for transfers between devices, plane(): return lax.ppermute(x, 'dp', pairs)  22.2 us
  transfers between devices with their start and end apart: 82, of which 23 were waited for; matrix products, arithmetic and copies ran while one was open for 12% of the time, Pallas kernels for 21%

profile of v2, /device:TPU:0, one launch (start us, length us, event | category | flops | bytes accessed | tf_op | source)
XLA Modules:
  0.0 461.3 jit_solution(16014643631612123448)
XLA Ops:
  6.3 4.7 %collective-permute-start.1 = (bf16[256,256]{0,1:T(8,128)(2,1)}, bf16[256,256]{0,1:T(8,128)(2,1)S(1)}, u32[]{:S(2)}, u32[]{:S(2)}) collective-permute-start(bf16[256,256]{0,1:T(8,128)(2,1)} %get-tuple-element.127), channel_id=1, source_target_pairs={{0,16},{8,24},{16,0},{24,8},{1,17},{9,25},{17,1},{25,9},{2,18},{10... | collective-permute-start | bytes 393224 | tf_op jit(solution)/shard_map/ppermute | solution.py:578
  13.3 5.4 %collective-permute-done.3 = f32[1,1024]{1,0:T(1,128)} collective-permute-done((f32[1,1024]{1,0:T(1,128)S(1)}, f32[1,1024]{1,0:T(1,128)}, u32[]{:S(2)}, u32[]{:S(2)}) %collective-permute-start.3) | collective-permute-done | bytes 4128 | tf_op jit(solution)/shard_map/ppermute | solution.py:578
  24.3 24.2 %collective-permute-done.2 = bf16[256,256]{0,1:T(8,128)(2,1)} collective-permute-done((bf16[256,256]{0,1:T(8,128)(2,1)}, bf16[256,256]{0,1:T(8,128)(2,1)}, u32[]{:S(2)}, u32[]{:S(2)}) %collective-permute-start.2) | collective-permute-done | bytes 131104 | tf_op jit(solution)/shard_map/ppermute | solution.py:578
  69.2 3.7 collective-permute-done.5.got_mate_ref
  78.3 4.1 feed_first.1
  97.9 5.2 %turn_weights.1 = (bf16[2816,1024]{1,0:T(8,128)(2,1)S(1)}, bf16[1536,1024]{1,0:T(8,128)(2,1)S(1)}) custom-call(bf16[1024,2816]{1,0:T(8,128)(2,1)} %bitcast.65, bf16[1024,1536]{1,0:T(8,128)(2,1)S(1)} %bitcast.54), custom_call_target="tpu_custom_call" | custom-call | flops 2281701376 | bytes 17825792 | tf_op jit(solution)/shard_map/turn_weights/pallas_call | solution.py:349
  113.3 3.8 collective-permute-done.37
  119.8 4.0 collective-permute-start.12
  130.9 5.8 %collective-permute-done.25 = bf16[256,1024]{1,0:T(8,128)(2,1)} collective-permute-done((bf16[256,1024]{1,0:T(8,128)(2,1)}, bf16[256,1024]{1,0:T(8,128)(2,1)}, u32[]{:S(2)}, u32[]{:S(2)}) %collective-permute-start.25) | collective-permute-done | bytes 524320 | tf_op jit(solution)/shard_map/ppermute | solution.py:578
  146.2 4.1 attn_second.1
  167.8 6.4 %feed_second.1 = (bf16[128,1024]{1,0:T(8,128)(2,1)S(1)}, bf16[128,1024]{1,0:T(8,128)(2,1)S(1)}, bf16[2,1024,128]{2,1,0:T(8,128)(2,1)S(1)}, f32[128,1024]{1,0:T(8,128)S(1)}, bf16[128,1024]{1,0:T(8,128)(2,1)S(1)}) custom-call(bf16[128,1024]{1,0:T(8,128)(2,1)} %get-tuple-element.56.own_ref.refs_1_, bf16[128,1024]{1,0:T(8,128)(2,1)} %collective-permute-done.14.mate_ref, ...), custom_call_target="tpu_custom_call" | custom-call | flops 6643777536 | bytes 11538432 | tf_op jit(solution)/shard_map/feed_second/pallas_call | solution.py:349
  174.3 8.8 %collective-permute-start.65 = (bf16[512,128]{1,0:T(8,128)(2,1)}, bf16[512,128]{1,0:T(8,128)(2,1)}, u32[]{:S(2)}, u32[]{:S(2)}) collective-permute-start(bf16[512,128]{1,0:T(8,128)(2,1)} %get-tuple-element.55), channel_id=1, source_target_pairs={{0,16},{8,24},{1,17},{9,25},{2,18},{10,26},{3,19},{11,27},{4,20},{... | collective-permute-start | bytes 393224 | tf_op jit(solution)/shard_map/ppermute | solution.py:578
  199.9 6.7 %attn_back.2 = (bf16[1024,128]{1,0:T(8,128)(2,1)S(1)}, bf16[128,1024]{1,0:T(8,128)(2,1)S(1)}, f32[1,1024]{1,0:T(1,128)S(1)}, f32[1,1024]{1,0:T(1,128)S(1)}, bf16...) custom-call(s32[2,4]{1,0:T(2,128)S(1)} %broadcast_select_fusion.23.ends_ref.refs_0_, ...), custom_call_target="tpu_custom_call" | custom-call | flops 2684354560 | bytes 10768416 | tf_op jit(solution)/shard_map/attn_back/pallas_call | solution.py:349
  210.6 8.2 %collective-permute-done.46.refs_10_.refs_5_ = bf16[1024,128]{1,0:T(8,128)(2,1)S(1)} collective-permute-done((bf16[1024,128]{1,0:T(8,128)(2,1)}, bf16[1024,128]{1,0:T(8,128)(2,1)S(1)}, u32[]{:S(2)}, u32[]{:S(2)}) %collective-permute-start.46) | collective-permute-done | bytes 262176 | tf_op jit(solution)/shard_map/ppermute | solution.py:584
  218.8 7.2 %collective-permute-start.75 = (bf16[1024,128]{1,0:T(8,128)(2,1)S(1)}, bf16[1024,128]{1,0:T(8,128)(2,1)S(1)}, u32[]{:S(2)}, u32[]{:S(2)}) collective-permute-start(bf16[1024,128]{1,0:T(8,128)(2,1)S(1)} %copy-done.39), channel_id=1, source_target_pairs={{0,6},{1,7},{2,0},{3,1},{4,2},{5,3},{6,4},{7,5},{8,14},{9,15},{10,... | collective-permute-start | bytes 786440 | tf_op jit(solution)/shard_map/ppermute | solution.py:584
  228.6 4.3 collective-permute-done.73.refs_13_
  245.1 4.6 feed_first_back.1
  251.0 21.1 %collective-permute-done.64 = bf16[512,128]{1,0:T(8,128)(2,1)S(1)} collective-permute-done((bf16[512,128]{1,0:T(8,128)(2,1)S(1)}, bf16[512,128]{1,0:T(8,128)(2,1)S(1)}, u32[]{:S(2)}, u32[]{:S(2)}) %collective-permute-start.64) | collective-permute-done | bytes 131104 | tf_op jit(solution)/shard_map/ppermute | solution.py:578
  274.6 4.1 collective-permute-start.58
  286.2 6.7 %collective-permute-done.22.refs_4_ = bf16[128,1024]{1,0:T(8,128)(2,1)S(1)} collective-permute-done((bf16[128,1024]{1,0:T(8,128)(2,1)S(1)}, bf16[128,1024]{1,0:T(8,128)(2,1)S(1)}, u32[]{:S(2)}, u32[]{:S(2)}) %collective-permute-start.22) | collective-permute-done | bytes 262176 | tf_op jit(solution)/shard_map/ppermute | solution.py:578
  295.4 3.9 collective-permute-done.60.refs_26_.refs_21_
  299.4 3.7 collective-permute-start.61
  303.1 6.1 %attn_back.3 = (bf16[1024,128]{1,0:T(8,128)(2,1)S(1)}, f32[128,1024]{1,0:T(8,128)S(1)}, f32[1,1024]{1,0:T(1,128)S(1)}, f32[1,1024]{1,0:T(1,128)S(1)}) custom-call(s32[2,4]{1,0:T(2,128)S(1)} %broadcast_select_fusion.23.ends_ref.refs_0_, bf16[128,1024]{1,0:T(8,128)(2,1)S(1)} %copy-done.29, bf16[128,1024]{1,0:T(8,128)(2,1)S(1)} %collective-permute-done.20.grad_own_ref.refs_2_, ...), custom_call_target="tpu_custom_call" | custom-call | flops 2684354560 | bytes 10768416 | tf_op jit(solution)/shard_map/attn_back/pallas_call | solution.py:349
  310.1 5.1 %collective-permute-start.67 = (bf16[2,512,128]{2,1,0:T(8,128)(2,1)S(1)}, bf16[2,512,128]{2,1,0:T(8,128)(2,1)S(1)}, u32[]{:S(2)}, u32[]{:S(2)}) collective-permute-start(bf16[2,512,128]{2,1,0:T(8,128)(2,1)S(1)} %pad_maximum_fusion.2.refs_30_), channel_id=1, source_target_pairs={{0,4},{1,5},{2,6},{3,7},{4,0},{5,1},{6,2},{7,3},{8,12},{9,13},{10,... | collective-permute-start | bytes 786440 | tf_op jit(solution)/shard_map/ppermute | solution.py:584
  322.5 30.1 %feed_weights.1 = (bf16[1024,2816]{1,0:T(8,128)(2,1)}, bf16[1408,1024]{1,0:T(8,128)(2,1)}) custom-call(s32[1]{0:T(128)} %bitcast.9.refs_0_, bf16[1024,128]{1,0:T(8,128)(2,1)S(1)} %copy-done.37, bf16[1024,128]{1,0:T(8,128)(2,1)S(1)} %copy-done.36, bf16[1024,128]{1,0:T(8,128)(2,1)S(1)} %collective-permute-done.44.refs_8_.refs_3_, ...), custom_call_target="tpu_custom_call" | custom-call | flops 17716740096 | bytes 16777216 | tf_op jit(solution)/shard_map/feed_weights/pallas_call | solution.py:532
  362.4 5.0 %collective-permute-done.50.refs_15_ = bf16[1024,128]{1,0:T(8,128)(2,1)S(1)} collective-permute-done((bf16[1024,128]{1,0:T(8,128)(2,1)S(1)}, bf16[1024,128]{1,0:T(8,128)(2,1)S(1)}, u32[]{:S(2)}, u32[]{:S(2)}) %collective-permute-start.50) | collective-permute-done | bytes 262176 | tf_op jit(solution)/shard_map/ppermute | solution.py:578
  368.0 5.0 %collective-permute-done.52.refs_17_ = bf16[1024,128]{1,0:T(8,128)(2,1)S(1)} collective-permute-done((bf16[1024,128]{1,0:T(8,128)(2,1)S(1)}, bf16[1024,128]{1,0:T(8,128)(2,1)S(1)}, u32[]{:S(2)}, u32[]{:S(2)}) %collective-permute-start.52) | collective-permute-done | bytes 262176 | tf_op jit(solution)/shard_map/ppermute | solution.py:578
  381.4 26.6 %attn_weights.1 = (bf16[1024,1536]{1,0:T(8,128)(2,1)}, bf16[512,1024]{1,0:T(8,128)(2,1)}) custom-call(s32[1]{0:T(128)} %bitcast.9.refs_0_, s32[8,4]{1,0:T(8,128)S(1)} %pad_add_fusion.refs_1_, bf16[2,1024,128]{2,1,0:T(8,128)(2,1)} %pad_maximum_fusion.1.refs_2_.refs_25_, bf16[2,1024,128]{2,1,0:T(8,128)(2,1)} %collective-permute-done.40.refs_3_.refs_26_, ...), custom_call_target="tpu_custom_call" | custom-call | flops 8589934592 | bytes 16777216 | tf_op jit(solution)/shard_map/attn_weights/pallas_call | solution.py:532
  410.8 5.3 %collective-permute-done.18 = bf16[128,256]{0,1:T(8,128)(2,1)S(1)} collective-permute-done((bf16[128,256]{0,1:T(8,128)(2,1)S(1)}, bf16[128,256]{0,1:T(8,128)(2,1)S(1)}, u32[]{:S(2)}, u32[]{:S(2)}) %collective-permute-start.18) | collective-permute-done | bytes 65568 | tf_op jit(solution)/shard_map/ppermute | solution.py:578
  439.9 6.7 %add_bitcast_fusion.2 = f32[1,1408,1024]{2,1,0:T(8,128)} fusion(bf16[1408,1024]{1,0:T(8,128)(2,1)} %collective-permute-done.78, bf16[1408,1024]{1,0:T(8,128)(2,1)} %get-tuple-element.90), kind=kLoop, calls=%fused_computation.2 | loop fusion | flops 4325376 | bytes 11534336 | tf_op jit(solution)/shard_map/broadcast_in_dim | solution.py:859
  446.7 5.6 %add_bitcast_fusion.1 = f32[1,1024,1536]{2,1,0:T(8,128)} fusion(bf16[1024,1536]{1,0:T(8,128)(2,1)} %collective-permute-done.69, bf16[1024,1536]{1,0:T(8,128)(2,1)S(1)} %copy-done.59), kind=kLoop, calls=%fused_computation.1 | loop fusion | flops 4718592 | bytes 12582912 | tf_op jit(solution)/shard_map/broadcast_in_dim | solution.py:859
  452.3 8.5 %add_bitcast_fusion = f32[1,1024,2816]{2,1,0:T(8,128)} fusion(bf16[1024,2816]{1,0:T(8,128)(2,1)} %collective-permute-done.77, bf16[1024,2816]{1,0:T(8,128)(2,1)S(1)} %bitcast.78), kind=kLoop, calls=%fused_computation | loop fusion | flops 8650752 | bytes 23068672 | tf_op jit(solution)/shard_map/broadcast_in_dim | solution.py:859
  (361 shorter events, 203.0 us)
Async XLA Ops:
  3.5 65.6 %collective-permute-start.8 = (bf16[512,1536]{1,0:T(8,128)(2,1)}, bf16[512,1536]{1,0:T(8,128)(2,1)}, u32[]{:S(2)}, u32[]{:S(2)}) collective-permute-start(bf16[512,1536]{1,0:T(8,128)(2,1)} %dynamic-slice_bitcast_fusion), channel_id=1, source_target_pairs={{16,24},{24,16},{17,25},{25,17},{18,26},{26,18},{19,27},{27,19},{2... | collective-permute-start | bytes 4718600 | tf_op jit(solution)/shard_map/ppermute | solution.py:578
  11.0 37.4 %collective-permute-start.2 = (bf16[256,256]{0,1:T(8,128)(2,1)}, bf16[256,256]{0,1:T(8,128)(2,1)}, u32[]{:S(2)}, u32[]{:S(2)}) collective-permute-start(bf16[256,256]{0,1:T(8,128)(2,1)} %get-tuple-element.127), channel_id=1, source_target_pairs={{0,24},{8,16},{16,8},{24,0},{1,25},{9,17},{17,9},{25,1},{2,26},{10... | collective-permute-start | bytes 393224 | tf_op jit(solution)/shard_map/ppermute | solution.py:578
  18.7 88.6 %collective-permute-start.39 = (s32[2,4]{1,0:T(2,128)S(1)}, s32[2,4]{1,0:T(2,128)}, u32[]{:S(2)}, u32[]{:S(2)}) collective-permute-start(s32[2,4]{1,0:T(2,128)S(1)} %broadcast_select_fusion.23.ends_ref.refs_0_), channel_id=1, source_target_pairs={{0,6},{1,7},{2,0},{3,1},{4,2},{5,3},{6,4},{7,5},{8,14},{9,15},{10,... | collective-permute-start | bytes 104 | tf_op jit(solution)/shard_map/ppermute | solution.py:584
  67.6 25.5 %collective-permute-start.10 = (bf16[256,1024]{1,0:T(8,128)(2,1)}, bf16[256,1024]{1,0:T(8,128)(2,1)}, u32[]{:S(2)}, u32[]{:S(2)}) collective-permute-start(bf16[256,1024]{1,0:T(8,128)(2,1)} %dynamic-slice_bitcast_fusion.1), channel_id=1, source_target_pairs={{16,24},{24,16},{17,25},{25,17},{18,26},{26,18},{19,27},{27,19},{2... | collective-permute-start | bytes 1572872 | tf_op jit(solution)/shard_map/ppermute | solution.py:578
  69.1 69.5 %collective-permute-start.9 = (bf16[512,1536]{1,0:T(8,128)(2,1)}, bf16[512,1536]{1,0:T(8,128)(2,1)}, u32[]{:S(2)}, u32[]{:S(2)}) collective-permute-start(bf16[512,1536]{1,0:T(8,128)(2,1)} %collective-permute-done.8), channel_id=1, source_target_pairs={{0,1},{1,0},{2,3},{3,2},{4,5},{5,4},{6,7},{7,6},{8,9},{9,8},{10,11... | collective-permute-start | bytes 4718600 | tf_op jit(solution)/shard_map/ppermute | solution.py:590
  87.4 58.8 %collective-permute-start.23 = (bf16[512,1536]{1,0:T(8,128)(2,1)}, bf16[512,1536]{1,0:T(8,128)(2,1)}, u32[]{:S(2)}, u32[]{:S(2)}) collective-permute-start(bf16[512,1536]{1,0:T(8,128)(2,1)} %constant_dynamic-slice_fusion.4), channel_id=1, source_target_pairs={{0,8},{8,0},{1,9},{9,1},{2,10},{10,2},{3,11},{11,3},{4,12},{12,4},... | collective-permute-start | bytes 4718600 | tf_op jit(solution)/shard_map/ppermute | solution.py:578
  93.1 32.6 %collective-permute-start.11 = (bf16[256,1024]{1,0:T(8,128)(2,1)}, bf16[256,1024]{1,0:T(8,128)(2,1)}, u32[]{:S(2)}, u32[]{:S(2)}) collective-permute-start(bf16[256,1024]{1,0:T(8,128)(2,1)} %collective-permute-done.10), channel_id=1, source_target_pairs={{0,1},{1,0},{2,3},{3,2},{4,5},{5,4},{6,7},{7,6},{8,9},{9,8},{10,11... | collective-permute-start | bytes 1572872 | tf_op jit(solution)/shard_map/ppermute | solution.py:590
  95.0 41.7 %collective-permute-start.25 = (bf16[256,1024]{1,0:T(8,128)(2,1)}, bf16[256,1024]{1,0:T(8,128)(2,1)}, u32[]{:S(2)}, u32[]{:S(2)}) collective-permute-start(bf16[256,1024]{1,0:T(8,128)(2,1)} %constant_dynamic-slice_fusion.3), channel_id=1, source_target_pairs={{0,8},{8,0},{1,9},{9,1},{2,10},{10,2},{3,11},{11,3},{4,12},{12,4},... | collective-permute-start | bytes 1572872 | tf_op jit(solution)/shard_map/ppermute | solution.py:578
  142.0 48.1 %collective-permute-start.40 = (bf16[2,1024,128]{2,1,0:T(8,128)(2,1)}, bf16[2,1024,128]{2,1,0:T(8,128)(2,1)}, u32[]{:S(2)}, u32[]{:S(2)}) collective-permute-start(bf16[2,1024,128]{2,1,0:T(8,128)(2,1)} %pad_maximum_fusion.1.refs_2_.refs_25_), channel_id=1, source_target_pairs={{0,2},{1,3},{2,4},{3,5},{4,6},{5,7},{6,0},{7,1},{8,10},{9,11},{10,... | collective-permute-start | bytes 1572872 | tf_op jit(solution)/shard_map/ppermute | solution.py:584
  143.6 50.7 %collective-permute-start.41 = (bf16[2,1024,128]{2,1,0:T(8,128)(2,1)}, bf16[2,1024,128]{2,1,0:T(8,128)(2,1)}, u32[]{:S(2)}, u32[]{:S(2)}) collective-permute-start(bf16[2,1024,128]{2,1,0:T(8,128)(2,1)} %pad_maximum_fusion.1.refs_2_.refs_25_), channel_id=1, source_target_pairs={{0,4},{1,5},{2,6},{3,7},{4,0},{5,1},{6,2},{7,3},{8,12},{9,13},{10,... | collective-permute-start | bytes 1572872 | tf_op jit(solution)/shard_map/ppermute | solution.py:584
  146.2 44.6 %collective-permute-start.24 = (bf16[512,1536]{1,0:T(8,128)(2,1)}, bf16[512,1536]{1,0:T(8,128)(2,1)}, u32[]{:S(2)}, u32[]{:S(2)}) collective-permute-start(bf16[512,1536]{1,0:T(8,128)(2,1)} %collective-permute-done.23), channel_id=1, source_target_pairs={{0,1},{1,0},{2,3},{3,2},{4,5},{5,4},{6,7},{7,6},{8,9},{9,8},{10,11... | collective-permute-start | bytes 4718600 | tf_op jit(solution)/shard_map/ppermute | solution.py:590
  154.9 40.4 %collective-permute-start.42 = (bf16[2,1024,128]{2,1,0:T(8,128)(2,1)}, bf16[2,1024,128]{2,1,0:T(8,128)(2,1)}, u32[]{:S(2)}, u32[]{:S(2)}) collective-permute-start(bf16[2,1024,128]{2,1,0:T(8,128)(2,1)} %pad_maximum_fusion.1.refs_2_.refs_25_), channel_id=1, source_target_pairs={{0,6},{1,7},{2,0},{3,1},{4,2},{5,3},{6,4},{7,5},{8,14},{9,15},{10,... | collective-permute-start | bytes 1572872 | tf_op jit(solution)/shard_map/ppermute | solution.py:584
  195.3 30.7 %collective-permute-start.48 = (bf16[1024,128]{1,0:T(8,128)(2,1)}, bf16[1024,128]{1,0:T(8,128)(2,1)S(1)}, u32[]{:S(2)}, u32[]{:S(2)}) collective-permute-start(bf16[1024,128]{1,0:T(8,128)(2,1)} %get-tuple-element.114.refs_6_.refs_1_), channel_id=1, source_target_pairs={{0,6},{1,7},{2,0},{3,1},{4,2},{5,3},{6,4},{7,5},{8,14},{9,15},{10,... | collective-permute-start | bytes 786440 | tf_op jit(solution)/shard_map/ppermute | solution.py:584
  198.2 29.1 %collective-permute-start.71 = (bf16[1024,128]{1,0:T(8,128)(2,1)}, bf16[1024,128]{1,0:T(8,128)(2,1)S(1)}, u32[]{:S(2)}, u32[]{:S(2)}) collective-permute-start(bf16[1024,128]{1,0:T(8,128)(2,1)} %get-tuple-element.110.refs_9_), channel_id=1, source_target_pairs={{0,2},{1,3},{2,4},{3,5},{4,6},{5,7},{6,0},{7,1},{8,10},{9,11},{10,... | collective-permute-start | bytes 786440 | tf_op jit(solution)/shard_map/ppermute | solution.py:584
  206.6 26.3 %collective-permute-start.73 = (bf16[1024,128]{1,0:T(8,128)(2,1)S(1)}, bf16[1024,128]{1,0:T(8,128)(2,1)S(1)}, u32[]{:S(2)}, u32[]{:S(2)}) collective-permute-start(bf16[1024,128]{1,0:T(8,128)(2,1)S(1)} %copy-done.39), channel_id=1, source_target_pairs={{0,4},{1,5},{2,6},{3,7},{4,0},{5,1},{6,2},{7,3},{8,12},{9,13},{10,... | collective-permute-start | bytes 786440 | tf_op jit(solution)/shard_map/ppermute | solution.py:584
  208.1 26.1 %collective-permute-start.27 = (bf16[512,128]{1,0:T(8,128)(2,1)S(1)}, bf16[512,128]{1,0:T(8,128)(2,1)S(1)}, u32[]{:S(2)}, u32[]{:S(2)}) collective-permute-start(bf16[512,128]{1,0:T(8,128)(2,1)S(1)} %get-tuple-element.69), channel_id=1, source_target_pairs={{16,0},{24,8},{17,1},{25,9},{18,2},{26,10},{19,3},{27,11},{20,4},{... | collective-permute-start | bytes 393224 | tf_op jit(solution)/shard_map/ppermute | solution.py:578
  239.9 34.7 %collective-permute-start.45 = (bf16[1024,128]{1,0:T(8,128)(2,1)S(1)}, bf16[1024,128]{1,0:T(8,128)(2,1)S(1)}, u32[]{:S(2)}, u32[]{:S(2)}) collective-permute-start(bf16[1024,128]{1,0:T(8,128)(2,1)S(1)} %collective-permute-done.44.refs_8_.refs_3_), channel_id=1, source_target_pairs={{0,8},{8,0},{16,24},{24,16},{1,9},{9,1},{17,25},{25,17},{2,10},{10... | collective-permute-start | bytes 786440 | tf_op jit(solution)/shard_map/ppermute | solution.py:578
  241.3 37.4 %collective-permute-start.47 = (bf16[1024,128]{1,0:T(8,128)(2,1)S(1)}, bf16[1024,128]{1,0:T(8,128)(2,1)S(1)}, u32[]{:S(2)}, u32[]{:S(2)}) collective-permute-start(bf16[1024,128]{1,0:T(8,128)(2,1)S(1)} %collective-permute-done.46.refs_10_.refs_5_), channel_id=1, source_target_pairs={{0,8},{8,0},{16,24},{24,16},{1,9},{9,1},{17,25},{25,17},{2,10},{10... | collective-permute-start | bytes 786440 | tf_op jit(solution)/shard_map/ppermute | solution.py:578
  243.0 39.1 %collective-permute-start.49 = (bf16[1024,128]{1,0:T(8,128)(2,1)S(1)}, bf16[1024,128]{1,0:T(8,128)(2,1)S(1)}, u32[]{:S(2)}, u32[]{:S(2)}) collective-permute-start(bf16[1024,128]{1,0:T(8,128)(2,1)S(1)} %collective-permute-done.48.refs_12_.refs_7_), channel_id=1, source_target_pairs={{0,8},{8,0},{16,24},{24,16},{1,9},{9,1},{17,25},{25,17},{2,10},{10... | collective-permute-start | bytes 786440 | tf_op jit(solution)/shard_map/ppermute | solution.py:578
  243.3 38.7 %collective-permute-start.72 = (bf16[1024,128]{1,0:T(8,128)(2,1)}, bf16[1024,128]{1,0:T(8,128)(2,1)S(1)}, u32[]{:S(2)}, u32[]{:S(2)}) collective-permute-start(bf16[1024,128]{1,0:T(8,128)(2,1)} %copy-done.46), channel_id=1, source_target_pairs={{0,8},{8,0},{16,24},{24,16},{1,9},{9,1},{17,25},{25,17},{2,10},{10... | collective-permute-start | bytes 786440 | tf_op jit(solution)/shard_map/ppermute | solution.py:578
  284.1 26.0 %collective-permute-start.76 = (bf16[1024,128]{1,0:T(8,128)(2,1)S(1)}, bf16[1024,128]{1,0:T(8,128)(2,1)S(1)}, u32[]{:S(2)}, u32[]{:S(2)}) collective-permute-start(bf16[1024,128]{1,0:T(8,128)(2,1)S(1)} %collective-permute-done.75.refs_15_), channel_id=1, source_target_pairs={{0,8},{8,0},{16,24},{24,16},{1,9},{9,1},{17,25},{25,17},{2,10},{10... | collective-permute-start | bytes 786440 | tf_op jit(solution)/shard_map/ppermute | solution.py:578
  310.1 42.5 %collective-permute-start.67 = (bf16[2,512,128]{2,1,0:T(8,128)(2,1)S(1)}, bf16[2,512,128]{2,1,0:T(8,128)(2,1)S(1)}, u32[]{:S(2)}, u32[]{:S(2)}) collective-permute-start(bf16[2,512,128]{2,1,0:T(8,128)(2,1)S(1)} %pad_maximum_fusion.2.refs_30_), channel_id=1, source_target_pairs={{0,4},{1,5},{2,6},{3,7},{4,0},{5,1},{6,2},{7,3},{8,12},{9,13},{10,... | collective-permute-start | bytes 786440 | tf_op jit(solution)/shard_map/ppermute | solution.py:584
  315.2 38.7 %collective-permute-start.68 = (bf16[2,512,128]{2,1,0:T(8,128)(2,1)S(1)}, bf16[2,512,128]{2,1,0:T(8,128)(2,1)S(1)}, u32[]{:S(2)}, u32[]{:S(2)}) collective-permute-start(bf16[2,512,128]{2,1,0:T(8,128)(2,1)S(1)} %pad_maximum_fusion.2.refs_30_), channel_id=1, source_target_pairs={{0,6},{1,7},{2,0},{3,1},{4,2},{5,3},{6,4},{7,5},{8,14},{9,15},{10,... | collective-permute-start | bytes 786440 | tf_op jit(solution)/shard_map/ppermute | solution.py:584
  318.6 40.8 %collective-permute-start.51 = (bf16[1024,128]{1,0:T(8,128)(2,1)S(1)}, bf16[1024,128]{1,0:T(8,128)(2,1)S(1)}, u32[]{:S(2)}, u32[]{:S(2)}) collective-permute-start(bf16[1024,128]{1,0:T(8,128)(2,1)S(1)} %get-tuple-element.81.refs_14_), channel_id=1, source_target_pairs={{0,2},{1,3},{2,4},{3,5},{4,6},{5,7},{6,0},{7,1},{8,10},{9,11},{10,... | collective-permute-start | bytes 786440 | tf_op jit(solution)/shard_map/ppermute | solution.py:584
  318.6 41.7 %collective-permute-start.53 = (bf16[1024,128]{1,0:T(8,128)(2,1)S(1)}, bf16[1024,128]{1,0:T(8,128)(2,1)S(1)}, u32[]{:S(2)}, u32[]{:S(2)}) collective-permute-start(bf16[1024,128]{1,0:T(8,128)(2,1)S(1)} %get-tuple-element.81.refs_14_), channel_id=1, source_target_pairs={{0,4},{1,5},{2,6},{3,7},{4,0},{5,1},{6,2},{7,3},{8,12},{9,13},{10,... | collective-permute-start | bytes 786440 | tf_op jit(solution)/shard_map/ppermute | solution.py:584
  319.2 42.3 %collective-permute-start.55 = (bf16[1024,128]{1,0:T(8,128)(2,1)S(1)}, bf16[1024,128]{1,0:T(8,128)(2,1)S(1)}, u32[]{:S(2)}, u32[]{:S(2)}) collective-permute-start(bf16[1024,128]{1,0:T(8,128)(2,1)S(1)} %get-tuple-element.81.refs_14_), channel_id=1, source_target_pairs={{0,6},{1,7},{2,0},{3,1},{4,2},{5,3},{6,4},{7,5},{8,14},{9,15},{10,... | collective-permute-start | bytes 786440 | tf_op jit(solution)/shard_map/ppermute | solution.py:584
  353.9 98.4 %collective-permute-start.77 = (bf16[1024,2816]{1,0:T(8,128)(2,1)}, bf16[1024,2816]{1,0:T(8,128)(2,1)}, u32[]{:S(2)}, u32[]{:S(2)}) collective-permute-start(bf16[1024,2816]{1,0:T(8,128)(2,1)} %get-tuple-element.89), channel_id=1, source_target_pairs={{0,1},{1,0},{2,3},{3,2},{4,5},{5,4},{6,7},{7,6},{8,9},{9,8},{10,11... | collective-permute-start | bytes 17301512 | tf_op jit(solution)/shard_map/ppermute | solution.py:590
  367.4 40.6 %collective-permute-start.35 = (f32[1,1152]{1,0:T(1,128)S(1)}, f32[1,1152]{1,0:T(1,128)S(1)}, u32[]{:S(2)}, u32[]{:S(2)}) collective-permute-start(f32[1,1152]{1,0:T(1,128)S(1)} %pad_maximum_fusion.3), channel_id=1, source_target_pairs={{0,6},{1,7},{2,0},{3,1},{4,2},{5,3},{6,4},{7,5},{8,14},{9,15},{10,... | collective-permute-start | bytes 13832 | tf_op jit(solution)/shard_map/ppermute | solution.py:584
  373.0 35.8 %collective-permute-start.34 = (f32[1,1152]{1,0:T(1,128)S(1)}, f32[1,1152]{1,0:T(1,128)S(1)}, u32[]{:S(2)}, u32[]{:S(2)}) collective-permute-start(f32[1,1152]{1,0:T(1,128)S(1)} %pad_maximum_fusion.3), channel_id=1, source_target_pairs={{0,4},{1,5},{2,6},{3,7},{4,0},{5,1},{6,2},{7,3},{8,12},{9,13},{10,... | collective-permute-start | bytes 13832 | tf_op jit(solution)/shard_map/ppermute | solution.py:584
  378.6 31.6 %collective-permute-start.33 = (f32[1,1152]{1,0:T(1,128)S(1)}, f32[1,1152]{1,0:T(1,128)S(1)}, u32[]{:S(2)}, u32[]{:S(2)}) collective-permute-start(f32[1,1152]{1,0:T(1,128)S(1)} %pad_maximum_fusion.3), channel_id=1, source_target_pairs={{0,2},{1,3},{2,4},{3,5},{4,6},{5,7},{6,0},{7,1},{8,10},{9,11},{10,... | collective-permute-start | bytes 13832 | tf_op jit(solution)/shard_map/ppermute | solution.py:584
  381.4 58.6 %collective-permute-start.78 = (bf16[1408,1024]{1,0:T(8,128)(2,1)}, bf16[1408,1024]{1,0:T(8,128)(2,1)}, u32[]{:S(2)}, u32[]{:S(2)}) collective-permute-start(bf16[1408,1024]{1,0:T(8,128)(2,1)} %get-tuple-element.90), channel_id=1, source_target_pairs={{0,1},{1,0},{2,3},{3,2},{4,5},{5,4},{6,7},{7,6},{8,9},{9,8},{10,11... | collective-permute-start | bytes 8650760 | tf_op jit(solution)/shard_map/ppermute | solution.py:590
  410.1 36.5 %collective-permute-start.69 = (bf16[1024,1536]{1,0:T(8,128)(2,1)}, bf16[1024,1536]{1,0:T(8,128)(2,1)}, u32[]{:S(2)}, u32[]{:S(2)}) collective-permute-start(bf16[1024,1536]{1,0:T(8,128)(2,1)} %get-tuple-element.85), channel_id=1, source_target_pairs={{0,1},{1,0},{2,3},{3,2},{4,5},{5,4},{6,7},{7,6},{8,9},{9,8},{10,11... | collective-permute-start | bytes 9437192 | tf_op jit(solution)/shard_map/ppermute | solution.py:590
  (123 other events, 1564.7 us)
